TPU v7x, 32 devices: a whole 2x2x4 slice. The times are simulated.
32 devices in a mesh: dp: 8 (over y, x, core), narrow: 4 (over z).
Axes of the slice: x: 2, y: 2, z: 4, core: 2. Of those that a mesh axis runs over, the one named last changes fastest.
Arguments:
- inputs: bfloat16 [16, 1152, 1024], P('dp', 'narrow'), may hold values from -6 to 6
- bucket: int32 [16], P('dp'), may hold values from 0 to 1, as said below
- attn_gain: bfloat16 [1024], P('dp'), may hold values from 0.5 to 1.5
- w_query: bfloat16 [1024, 1024], P('dp', 'narrow'), may hold values from -0.1875 to 0.1875
- w_key: bfloat16 [1024, 1024], P('dp', 'narrow'), may hold values from -0.1875 to 0.1875
- w_value: bfloat16 [1024, 1024], P('dp', 'narrow'), may hold values from -0.1875 to 0.1875
- w_out: bfloat16 [1024, 1024], P('narrow', 'dp'), may hold values from -6 to 6
- ffn_gain: bfloat16 [1024], P('dp'), may hold values from 0.5 to 1.5
- w_gate: bfloat16 [1024, 2816], P('dp', 'narrow'), may hold values from -0.1875 to 0.1875
- w_up: bfloat16 [1024, 2816], P('dp', 'narrow'), may hold values from -0.1875 to 0.1875
- w_down: bfloat16 [2816, 1024], P('narrow', 'dp'), may hold values from -0.109375 to 0.109375
- cotangent: bfloat16 [16, 1152, 1024], P('dp', 'narrow'), may hold values from -6 to 6
Outputs:
- outputs: bfloat16 [16, 1152, 1024], P('dp', 'narrow')
- input_grad: float32 [16, 1152, 1024], P('dp', 'narrow')
- attn_gain_grad: float32 [1024], P('dp')
- w_query_grad: float32 [1024, 1024], P('dp', 'narrow')
- w_key_grad: float32 [1024, 1024], P('dp', 'narrow')
- w_value_grad: float32 [1024, 1024], P('dp', 'narrow')
- w_out_grad: float32 [1024, 1024], P('narrow', 'dp')
- ffn_gain_grad: float32 [1024], P('dp')
- w_gate_grad: float32 [1024, 2816], P('dp', 'narrow')
- w_up_grad: float32 [1024, 2816], P('dp', 'narrow')
- w_down_grad: float32 [2816, 1024], P('narrow', 'dp')
Inputs may be any that keep to these rules, and one draw needn't show every extreme that they name: `bucket`: 1 marks a group holding one row of 1152 positions (448 px), 0 a group of three rows of 384 positions (224 px); both kinds occur in every draw.
All inputs are finite; a program needn't handle non-finite values.
Results may differ from a plain program's by a relative error of at most 0.017.
Values may be sent and summed in bfloat16 or wider, within the bound.
No kernel may reach another device: no remote copies, remote signals or barrier semaphores. Data moves between devices by JAX's collectives and lax.ppermute only.
A program may use at most 256 MiB of HBM per device.

v0:
```python
import functools

import jax
import jax.numpy as jnp
from jax import lax
from jax.experimental import pallas as pl
from jax.experimental.pallas import tpu as pltpu
from jax.sharding import PartitionSpec as P

HEAD = 64
SHORT = 384
EPS = 1e-06
BLOCKS = 4
f32 = jnp.float32
bf16 = jnp.bfloat16


def dot_nn(left, right):
    return jnp.dot(left, right, preferred_element_type=f32)


def dot_nt(left, right):
    return lax.dot_general(left, right, (((1,), (1,)), ((), ())), preferred_element_type=f32)


def call(kernel, grid, prefetch, in_specs, out_specs, out_shape, scratch, flops, moved, vmem):
    return pl.pallas_call(
        kernel,
        grid_spec=pltpu.PrefetchScalarGridSpec(
            num_scalar_prefetch=prefetch,
            grid=grid,
            in_specs=in_specs,
            out_specs=out_specs,
            scratch_shapes=scratch,
        ),
        out_shape=out_shape,
        compiler_params=pltpu.CompilerParams(vmem_limit_bytes=vmem << 20),
        cost_estimate=pl.CostEstimate(flops=flops, bytes_accessed=moved, transcendentals=0),
    )


def shaped(shape, dtype):
    return jax.ShapeDtypeStruct(shape, dtype)


def rms_of(rows):
    return lax.rsqrt(jnp.mean(rows * rows, axis=-1, keepdims=True) + EPS)


def store_grad(refs, step, grad, first):
    x_keep, x_send, y_keep, y_send = refs
    half, rows = grad.shape[0] // 2, slice(first, first + grad.shape[1])
    (x_send if step % 2 else x_keep)[step // 2, :, rows] = grad[:half]
    (y_send if step // 2 else y_keep)[step % 2, :, rows] = grad[half:]


def grad_shapes(pieces, rows, wide):
    return [shaped((2, pieces // 2, rows, wide), bf16)] * 4


def square_split_kernel(
    core_ref, bucket_ref, q_ref, k_ref, v_ref, o_ref, attn_ref, ffn_ref, keep_ref, give_ref
):
    halves = [ref[...].T for ref in (q_ref, k_ref, v_ref)] + [o_ref[...]]
    shape = (16, keep_ref.shape[1])
    row, lane = (lax.broadcasted_iota(jnp.int32, shape, axis) for axis in range(2))
    flags = jnp.zeros(shape, f32)
    for i in range(bucket_ref.shape[0]):
        flags = jnp.where(lane == i, bucket_ref[i].astype(f32), flags)
    flags = jnp.where(row == 2, flags, 0.0)
    flags = jnp.where(row == 1, ffn_ref[...].astype(f32), flags)
    extra = jnp.where(row == 0, attn_ref[...].astype(f32), flags).astype(bf16)

    def store(low_ref, high_ref):
        start = 0
        for half in halves:
            count = half.shape[0] // 2
            low_ref[start : start + count] = half[:count]
            high_ref[start : start + count] = half[count:]
            start += count
        low_ref[start:] = extra
        high_ref[start:] = extra

    @pl.when(core_ref[0] == 0)
    def _():
        store(keep_ref, give_ref)

    @pl.when(core_ref[0] != 0)
    def _():
        store(give_ref, keep_ref)


def square_split_call(core, bucket, q, k, v, o, attn, ffn):
    rows, cols = q.shape[1] // 2 * 4 + 16, o.shape[1]
    whole = pl.BlockSpec(memory_space=pltpu.VMEM)
    return call(
        square_split_kernel,
        (),
        2,
        [whole] * 6,
        [whole] * 2,
        [shaped((rows, cols), bf16)] * 2,
        [],
        0,
        1 << 20,
        16,
    )(core, bucket, q, k, v, o, attn[None], ffn[None])


def ffn_split_kernel(cut, core_ref, *refs):
    parts, (keep_ref, give_ref) = refs[:3], refs[3:]

    def store(low_ref, high_ref):
        start = 0
        half = parts[0].shape[0] // 2
        for first, last in ((0, cut), (cut, half)):
            for part in parts:
                count = last - first
                low_ref[start : start + count] = part[first:last]
                high_ref[start : start + count] = part[half + first : half + last]
                start += count

    @pl.when(core_ref[0] == 0)
    def _():
        store(keep_ref, give_ref)

    @pl.when(core_ref[0] != 0)
    def _():
        store(give_ref, keep_ref)


def ffn_split_call(core, cut, gate, up, down):
    rows, cols = gate.shape[0] // 2 * 3, gate.shape[1]
    whole = pl.BlockSpec(memory_space=pltpu.VMEM)
    return call(
        functools.partial(ffn_split_kernel, cut),
        (),
        1,
        [whole] * 3,
        [whole] * 2,
        [shaped((rows, cols), bf16)] * 2,
        [],
        0,
        1 << 20,
        16,
    )(core, gate, up, down)


def join_rows(core_ref, own_ref, other_ref, out_ref):
    count = own_ref.shape[1]

    @pl.when(core_ref[0] == 0)
    def _():
        out_ref[:count] = own_ref[0]
        out_ref[count:] = other_ref[0]

    @pl.when(core_ref[0] != 0)
    def _():
        out_ref[:count] = other_ref[0]
        out_ref[count:] = own_ref[0]


def qkv_kernel(
    me_ref, core_ref, place_ref, own_ref, other_ref, w_ref, x_ref, hidden_ref, rms_ref, gains_ref, q_ref, k_ref, v_ref
):
    join_rows(core_ref, own_ref, other_ref, x_ref)
    rows = x_ref[...].astype(f32)
    rms = rms_of(rows)
    rms_ref[...] = jnp.broadcast_to(rms, rms_ref.shape)
    wide = w_ref.shape[3]
    half = w_ref.shape[1] * 128
    for step in range(BLOCKS):
        columns = pl.ds(pl.multiple_of((me_ref[0] ^ step) * wide, wide), wide)
        gains = w_ref[step, 0, 4 * 128 :, :].astype(f32)
        gains_ref[:, columns] = gains[:8]
        hidden_ref[:, columns] = (x_ref[:, columns].astype(f32) * rms * gains[:1]).astype(bf16)
    for part, ref in enumerate((q_ref, k_ref, v_ref)):
        total = None
        for step in range(BLOCKS):
            start = pl.multiple_of((me_ref[0] ^ step) * wide, wide)
            weight = w_ref[step, :, part * 128 : (part + 1) * 128, :].reshape(half, wide)
            piece = dot_nt(hidden_ref[:, pl.ds(start, wide)], weight)
            total = piece if total is None else total + piece
        if part == 0:
            total = total * (HEAD**-0.5)
        ref[...] = total.astype(bf16)


def qkv_call(me, core, place, own, other, weights):
    places, half_tile, width = own.shape
    half = weights.shape[1] * 128
    tile, count = 2 * half_tile, 2 * half_tile * places
    row_spec = pl.BlockSpec((tile, width), lambda i, me, core, place: (i, 0))
    half_spec = pl.BlockSpec((tile, half), lambda i, me, core, place: (i, 0))
    part_spec = pl.BlockSpec(
        (1, half_tile, width), lambda i, me, core, place: ((place[0] + places - i) % places, 0, 0)
    )
    return call(
        qkv_kernel,
        (places,),
        3,
        [
            part_spec,
            part_spec,
            pl.BlockSpec(weights.shape, lambda i, me, core, place: (0, 0, 0, 0)),
        ],
        [
            row_spec,
            row_spec,
            pl.BlockSpec((tile, 128), lambda i, me, core, place: (i, 0)),
            pl.BlockSpec((8, width), lambda i, me, core, place: (0, 0)),
            half_spec,
            half_spec,
            half_spec,
        ],
        [shaped((count, width), bf16)] * 2
        + [shaped((count, 128), f32), shaped((8, width), f32)]
        + [shaped((count, half), bf16)] * 3,
        [],
        2 * count * width * half * 3,
        12 << 20,
        40,
    )(me, core, place, own, other, weights)


def two_heads(rows):
    low = lax.broadcasted_iota(jnp.int32, rows.shape, 1) < HEAD
    zero = jnp.zeros_like(rows)
    return jnp.concatenate([jnp.where(low, rows, zero), jnp.where(low, zero, rows)], axis=0)


def one_pair(both):
    half = both.shape[1] // 2
    return jnp.concatenate([both[:HEAD, :half], both[HEAD:, half:]], axis=0)


def attend_kernel(flag_ref, q_ref, k_ref, v_ref, out_ref, probs_ref, v_turned):
    block = pl.program_id(1)

    @pl.when(block == 0)
    def _():
        v_turned[...] = v_ref[...].T

    queries = two_heads(q_ref[...])

    def attend(keys, values):
        scores = dot_nt(keys, queries)
        expo = jnp.exp(scores - jnp.max(scores, axis=0, keepdims=True))
        probs = (expo * (1.0 / jnp.sum(expo, axis=0, keepdims=True))).astype(bf16)
        probs_ref[0, 0, : keys.shape[0], :] = probs
        out_ref[...] = one_pair(dot_nn(values, probs)).T.astype(bf16)

    @pl.when(flag_ref[0] == 1)
    def _():
        attend(k_ref[...], v_turned[...])

    @pl.when(flag_ref[0] != 1)
    def _():
        start = pl.multiple_of(block * SHORT, SHORT)
        attend(k_ref[pl.ds(start, SHORT), :], v_turned[:, pl.ds(start, SHORT)])


def attend_call(flag, q, k, v):
    count, half = q.shape
    pairs, blocks = half // 128, count // SHORT
    some = pl.BlockSpec((SHORT, 128), lambda j, i, flag: (i, j))
    every = pl.BlockSpec((count, 128), lambda j, i, flag: (0, j))
    return call(
        attend_kernel,
        (pairs, blocks),
        1,
        [some, every, every],
        [some, pl.BlockSpec((1, 1, count, 2 * SHORT), lambda j, i, flag: (j, i, 0, 0))],
        [shaped(q.shape, bf16), shaped((pairs, blocks, count, 2 * SHORT), bf16)],
        [pltpu.VMEM((128, count), bf16)],
        4 * 4 * count * count * half,
        28 << 20,
        48,
    )(flag, q, k, v)


def branch_kernel(me_ref, att_ref, w_ref, out_ref):
    wide = w_ref.shape[3]
    for step in range(BLOCKS):
        start = pl.multiple_of((me_ref[0] ^ step) * wide, wide)
        weight = w_ref[step].reshape(att_ref.shape[1], wide)
        out_ref[:, pl.ds(start, wide)] = dot_nn(att_ref[...], weight).astype(bf16)


def branch_call(me, attended, weights):
    count, half = attended.shape
    width = weights.shape[0] * weights.shape[3]
    tile = count // 4
    block = weights.shape[:2] + (128,) + weights.shape[3:]
    return call(
        branch_kernel,
        (count // tile,),
        1,
        [
            pl.BlockSpec((tile, half), lambda i, me: (i, 0)),
            pl.BlockSpec(block, lambda i, me: (0, 0, 3, 0)),
        ],
        pl.BlockSpec((tile, width), lambda i, me: (i, 0)),
        shaped((count, width), bf16),
        [],
        2 * count * width * half,
        5 << 20,
        24,
    )(me, attended, weights)


def middle_kernel(
    core_ref, place_ref, x_ref, one_ref, two_ref, gain_ref, own_ref, other_ref, middle_ref, normed_ref, cot_ref
):
    middle = x_ref[...].astype(f32) + (one_ref[...].astype(f32) + two_ref[...].astype(f32))
    middle_ref[...] = middle
    normed_ref[...] = (middle * rms_of(middle) * gain_ref[1:2, :]).astype(bf16)
    join_rows(core_ref, own_ref, other_ref, cot_ref)


def middle_call(core, place, rows, one, two, gain, own, other):
    count, width = rows.shape
    places, half_tile = own.shape[:2]
    spec = pl.BlockSpec((2 * half_tile, width), lambda i, core, place: (i, 0))
    part_spec = pl.BlockSpec(
        (1, half_tile, width), lambda i, core, place: ((place[0] + places - i) % places, 0, 0)
    )
    return call(
        middle_kernel,
        (places,),
        2,
        [spec] * 3
        + [pl.BlockSpec((8, width), lambda i, core, place: (0, 0)), part_spec, part_spec],
        [spec] * 3,
        [shaped(rows.shape, f32), shaped(rows.shape, bf16), shaped(rows.shape, bf16)],
        [],
        0,
        14 << 20,
        32,
    )(core, place, rows, one, two, gain, own, other)


def ffn_kernel(given, prior, me_ref, normed_ref, d_out_ref, *refs):
    pieces_of, refs = refs[:given], refs[given:]
    before = refs[:2] if prior else None
    refs = refs[2 if prior else 0 :]
    result_ref, d_normed_ref = refs[:2]
    grad_refs = refs[2:6]
    weights, inner_t, gate_t, up_t = refs[6:]
    pieces, rows_all, wide = pieces_of[0].shape
    parts, kinds, depth = BLOCKS, 3, rows_all // 3
    units = pieces * depth
    tile = SHORT

    def columns(step):
        return pl.ds(pl.multiple_of((me_ref[0] ^ step) * wide, wide), wide)

    for kind in range(kinds):
        rows = slice(kind * depth, (kind + 1) * depth)
        for step in range(parts):
            start = 0
            for piece in pieces_of[step:] if step == parts - 1 else pieces_of[step : step + 1]:
                count = piece.shape[0] * depth
                value = piece[:, rows, :].reshape(count, wide)
                weights[kind, start : start + count, columns(step)] = value
                start += count

    def rows_step(index, carry):
        rows = pl.ds(pl.multiple_of(index * tile, tile), tile)
        normed = normed_ref[rows, :]
        gate, up = dot_nt(normed, weights[0]), dot_nt(normed, weights[1])
        d_inner = dot_nt(d_out_ref[rows, :], weights[2])
        square = gate * gate
        bent = jnp.tanh(gate * (0.7978845608 + 0.7978845608 * 0.044715 * square))
        half = 0.5 + 0.5 * bent
        gelu = gate * half
        slope = half + gate * (0.5 - 0.5 * bent * bent) * (
            0.7978845608 + 0.7978845608 * 3 * 0.044715 * square
        )
        inner = (gelu * up).astype(bf16)
        d_gate = (d_inner * up * slope).astype(bf16)
        d_up = (d_inner * gelu).astype(bf16)
        inner_t[:, rows] = inner.T
        gate_t[:, rows] = d_gate.T
        up_t[:, rows] = d_up.T
        forward = dot_nn(inner, weights[2])
        backward = dot_nn(d_gate, weights[0]) + dot_nn(d_up, weights[1])
        if prior:
            forward += before[0][rows, :].astype(f32)
            backward += before[1][rows, :].astype(f32)
        result_ref[rows, :] = forward.astype(bf16)
        d_normed_ref[rows, :] = backward.astype(bf16)
        return carry

    lax.fori_loop(0, normed_ref.shape[0] // tile, rows_step, 0)
    for step in range(parts):
        here, there = normed_ref[:, columns(step)], d_out_ref[:, columns(step)]
        for kind, (left, right) in enumerate(((gate_t, here), (up_t, here), (inner_t, there))):
            grad = dot_nn(left[...], right).astype(bf16)
            store_grad(grad_refs, step, grad.reshape(pieces, depth, wide), kind * depth)


def ffn_call(me, normed, d_out, weights, *before):
    count, width = normed.shape
    pieces, rows_all, wide = weights[0].shape
    units = pieces * rows_all // 3
    whole = pl.BlockSpec(memory_space=pltpu.VMEM)
    return call(
        functools.partial(ffn_kernel, len(weights), bool(before)),
        (),
        1,
        [whole] * (2 + len(weights) + len(before)),
        [whole] * 6,
        [shaped(normed.shape, bf16)] * 2 + grad_shapes(pieces, rows_all, wide),
        [pltpu.VMEM((3, units, width), bf16)] + [pltpu.VMEM((units, count), bf16)] * 3,
        18 * count * width * units,
        20 << 20,
        56,
    )(me, normed, d_out, *weights, *before)


def turn_kernel(
    me_ref,
    core_ref,
    middle_ref,
    one_ref,
    two_ref,
    cot_ref,
    gain_ref,
    w_ref,
    own_ref,
    other_ref,
    d_middle_ref,
    d_branch_ref,
    d_att_ref,
    gain_grad_ref,
    out_ref,
):
    middle = middle_ref[...]
    rms = rms_of(middle)
    scaled = middle * rms
    d_normed = one_ref[...].astype(f32) + two_ref[...].astype(f32)
    pulled = d_normed * gain_ref[1:2, :]
    d_middle = cot_ref[...].astype(f32) + rms * (
        pulled - scaled * jnp.mean(pulled * scaled, axis=-1, keepdims=True)
    )
    d_middle_ref[...] = d_middle
    d_branch_ref[...] = d_middle.astype(bf16)
    count = out_ref.shape[1]
    rows = pl.ds(pl.multiple_of(core_ref[0] * count, count), count)
    out_ref[0] = (
        middle_ref[rows, :] + (own_ref[0, 0].astype(f32) + other_ref[0].astype(f32))
    ).astype(bf16)

    @pl.when(pl.program_id(0) == 0)
    def _():
        gain_grad_ref[...] = jnp.zeros_like(gain_grad_ref)

    gain_grad_ref[...] += jnp.sum(d_normed * scaled, axis=0, keepdims=True)
    wide = w_ref.shape[3]
    total = None
    for step in range(BLOCKS):
        start = pl.multiple_of((me_ref[0] ^ step) * wide, wide)
        piece = dot_nt(d_branch_ref[:, pl.ds(start, wide)], w_ref[step].reshape(d_att_ref.shape[1], wide))
        total = piece if total is None else total + piece
    d_att_ref[...] = total.astype(bf16)


def turn_call(me, core, middle, one, two, cot, gain, weights, own, other):
    count, width = middle.shape
    half = weights.shape[1] * 128
    places, _, half_tile, _ = own.shape
    tile = 2 * half_tile
    spec = pl.BlockSpec((tile, width), lambda i, me, core: (i, 0))
    line = pl.BlockSpec((1, width), lambda i, me, core: (0, 0))
    gain_spec = pl.BlockSpec((8, width), lambda i, me, core: (0, 0))
    plain = pl.BlockSpec((1, half_tile, width), lambda i, me, core: (i, 0, 0))
    block = weights.shape[:2] + (128,) + weights.shape[3:]
    return call(
        turn_kernel,
        (places,),
        2,
        [spec, spec, spec, spec, gain_spec]
        + [pl.BlockSpec(block, lambda i, me, core: (0, 0, 3, 0))]
        + [pl.BlockSpec((1, 1, half_tile, width), lambda i, me, core: (i, core[0], 0, 0)), plain],
        [spec, spec, pl.BlockSpec((tile, half), lambda i, me, core: (i, 0)), line, plain],
        [
            shaped(middle.shape, f32),
            shaped(middle.shape, bf16),
            shaped((count, half), bf16),
            shaped((1, width), f32),
            shaped((places, half_tile, width), bf16),
        ],
        [],
        2 * count * width * half,
        22 << 20,
        40,
    )(me, core, middle, one, two, cot, gain, weights, own, other)


def attend_back_kernel(
    flag_ref, q_ref, k_ref, v_ref, out_ref, d_out_ref, probs_ref, dq_ref, dk_ref, dv_ref, k_turned, dk_sum, dv_sum
):
    block, blocks = pl.program_id(1), pl.num_programs(1)

    @pl.when(block == 0)
    def _():
        k_turned[...] = k_ref[...].T

    queries, grads = two_heads(q_ref[...]), two_heads(d_out_ref[...])
    turned = (d_out_ref[...].astype(f32) * out_ref[...].astype(f32)).T
    delta = jnp.concatenate(
        [
            jnp.sum(turned[:HEAD], axis=0, keepdims=True),
            jnp.sum(turned[HEAD:], axis=0, keepdims=True),
        ],
        axis=1,
    )

    def back(values, keys_turned):
        probs = probs_ref[0, 0, : values.shape[0], :]
        d_probs = dot_nt(values, grads)
        d_scores = (probs.astype(f32) * (d_probs - delta)).astype(bf16)
        d_query = one_pair(dot_nn(keys_turned, d_scores)).T * (HEAD**-0.5)
        dq_ref[...] = d_query.astype(bf16)
        return dot_nn(d_scores, queries), dot_nn(probs, grads)

    @pl.when(flag_ref[0] == 1)
    def _():
        d_key, d_value = back(v_ref[...], k_turned[...])

        @pl.when(block == 0)
        def _():
            dk_sum[...] = d_key
            dv_sum[...] = d_value

        @pl.when(block > 0)
        def _():
            dk_sum[...] += d_key
            dv_sum[...] += d_value

    @pl.when(flag_ref[0] != 1)
    def _():
        rows = pl.ds(pl.multiple_of(block * SHORT, SHORT), SHORT)
        d_key, d_value = back(v_ref[rows, :], k_turned[:, rows])
        dk_sum[rows, :] = d_key
        dv_sum[rows, :] = d_value

    @pl.when(block == blocks - 1)
    def _():
        dk_ref[...] = dk_sum[...].astype(bf16)
        dv_ref[...] = dv_sum[...].astype(bf16)


def attend_back_call(flag, q, k, v, out, d_out, probs):
    count, half = q.shape
    pairs, blocks = half // 128, count // SHORT
    some = pl.BlockSpec((SHORT, 128), lambda j, i, flag: (i, j))
    every = pl.BlockSpec((count, 128), lambda j, i, flag: (0, j))
    return call(
        attend_back_kernel,
        (pairs, blocks),
        1,
        [
            some,
            every,
            every,
            some,
            some,
            pl.BlockSpec((1, 1, count, 2 * SHORT), lambda j, i, flag: (j, i, 0, 0)),
        ],
        [some, every, every],
        [shaped(q.shape, bf16)] * 3,
        [pltpu.VMEM((128, count), bf16)] + [pltpu.VMEM((count, 128), f32)] * 2,
        4 * 8 * count * count * half,
        30 << 20,
        48,
    )(flag, q, k, v, out, d_out, probs)


def square_kernel(
    me_ref, dq_ref, dk_ref, dv_ref, att_ref, hidden_ref, d_branch_ref, w_ref, x_ref, rms_ref, line_ref, d_hidden_ref, *refs
):
    grad_refs, turned = refs[:4], refs[4]
    lefts = (dq_ref, dk_ref, dv_ref, att_ref)

    @pl.when(pl.program_id(0) == 0)
    def _():
        for part, ref in enumerate(lefts):
            turned[part] = ref[...].T

    pieces, wide = w_ref.shape[1], w_ref.shape[3]

    def put(grad, first):
        for step in range(BLOCKS):

            @pl.when(pl.program_id(0) == step)
            def _():
                store_grad(grad_refs, step, grad, first)

    total = None
    for part, ref in enumerate(lefts):
        rows = slice(part * 128, (part + 1) * 128)
        right = d_branch_ref if part == 3 else hidden_ref
        grad = dot_nn(turned[part], right[...])
        put(grad.reshape(pieces, 128, wide).astype(bf16), part * 128)
        if part < 3:
            piece = dot_nn(ref[...], w_ref[0, :, rows, :].reshape(pieces * 128, wide))
            total = piece if total is None else total + piece
    d_hidden_ref[...] = total.astype(bf16)
    scaled = x_ref[...].astype(f32) * rms_ref[:, :1]
    attn = jnp.sum(total * scaled, axis=0, keepdims=True)
    lines = jnp.concatenate([attn, line_ref[...], jnp.zeros((14, wide), f32)], axis=0).astype(bf16)
    put(jnp.broadcast_to(lines[None], (pieces, 16, wide)), 4 * 128)


def square_call(me, dq, dk, dv, attended, hidden, d_branch, weights, x_rows, rms, line):
    count, half = dq.shape
    width = hidden.shape[1]
    parts, pieces, depth, wide = weights.shape
    every = pl.BlockSpec((count, half), lambda d, me: (0, 0))
    column = pl.BlockSpec((count, wide), lambda d, me: (0, me[0] ^ d))
    return call(
        square_kernel,
        (parts,),
        1,
        [every] * 4
        + [column, column, pl.BlockSpec((1, pieces, depth, wide), lambda d, me: (d, 0, 0, 0))]
        + [column, pl.BlockSpec(rms.shape, lambda d, me: (0, 0))]
        + [pl.BlockSpec((1, wide), lambda d, me: (0, me[0] ^ d))],
        [column] + [pl.BlockSpec((2, pieces // 2, depth, wide), lambda d, me: (0, 0, 0, 0))] * 4,
        [shaped(hidden.shape, bf16)] + grad_shapes(pieces, depth, wide),
        [pltpu.VMEM((4, half, count), bf16)],
        14 * count * width * half,
        24 << 20,
        40,
    )(me, dq, dk, dv, attended, hidden, d_branch, weights, x_rows, rms, line)


def input_kernel(core_ref, x_ref, d_middle_ref, own_ref, other_ref, gain_ref, out_ref):
    rows = x_ref[0, 0].astype(f32)
    rms = rms_of(rows)
    scaled = rows * rms
    d_hidden = own_ref[0, 0].astype(f32) + other_ref[0].astype(f32)
    pulled = d_hidden * gain_ref[:1, :]
    out_ref[0] = (
        d_middle_ref[0, 0]
        + rms * (pulled - scaled * jnp.mean(pulled * scaled, axis=-1, keepdims=True))
    ).astype(bf16)


def input_call(core, rows, d_middle, own, other, gains):
    slots, halves, tile, width = own.shape
    mine = pl.BlockSpec((1, 1, tile, width), lambda i, core: (i, core[0], 0, 0))
    plain = pl.BlockSpec((1, tile, width), lambda i, core: (i, 0, 0))
    return call(
        input_kernel,
        (slots,),
        1,
        [mine, mine, mine, plain, pl.BlockSpec((8, width), lambda i, core: (0, 0))],
        plain,
        shaped((slots, tile, width), bf16),
        [],
        0,
        8 << 20,
        16,
    )(core, rows.reshape(own.shape), d_middle.reshape(own.shape), own, other, gains)


def per_device(
    inputs,
    bucket,
    attn_gain,
    w_query,
    w_key,
    w_value,
    w_out,
    ffn_gain,
    w_gate,
    w_up,
    w_down,
    cotangent,
):
    dp, narrow = lax.axis_size("dp"), lax.axis_size("narrow")
    chips = dp // 2
    core, chip = lax.axis_index("dp") % 2, lax.axis_index("dp") // 2
    place = lax.axis_index("narrow")
    same_core = [[2 * m + c for m in range(chips)] for c in range(2)]
    by_core = core == 0
    bundle, row_count, width = inputs.shape
    tile = row_count // 2
    own_width = w_query.shape[0]
    wide = width // BLOCKS

    def to_core(value):
        return lax.ppermute(value, "dp", [(i, i ^ 1) for i in range(dp)])

    def to_chip(value, flip):
        return lax.ppermute(value, "dp", [(i, i ^ (2 * flip)) for i in range(dp)])

    def along(value, shift):
        return lax.ppermute(
            value, "narrow", [(i, (i + shift) % narrow) for i in range(narrow)]
        )

    def stage(values, *done):
        return lax.optimization_barrier((values, done))[0]

    def ordered(mine, theirs, axis):
        join = functools.partial(jnp.concatenate, axis=axis)
        return jnp.where(by_core, join([mine, theirs]), join([theirs, mine]))

    def pick(value, index, axis):
        return lax.dynamic_index_in_dim(value, index, axis, keepdims=False)

    def mine_of(value, axis):
        low, high = (lax.index_in_dim(value, i, axis, keepdims=False) for i in range(2))
        return jnp.where(by_core, low, high), jnp.where(by_core, high, low)

    def turn(k):
        return lax.rem(place + (k + narrow), narrow)

    def blocks_for(value):
        return [pick(value, turn(k), 0) for k in range(narrow)]

    def across(blocks, *late):
        moved = [blocks[0]]
        for k in range(1, narrow):
            block = stage(blocks[k], *late) if late and 2 * k == narrow else blocks[k]
            moved.append(along(block, k))
        return moved

    def in_order(moved):
        stacked = jnp.stack(moved)
        return jnp.stack([pick(stacked, turn(-i), 0) for i in range(narrow)])

    def group_start(value):
        keep, give = mine_of(value.reshape(bundle, 2, tile, width), 1)
        return ordered(keep, to_core(give), 0)

    def group_back(moved):
        mine, give = mine_of(in_order(moved).reshape(2, bundle, tile, width), 0)
        theirs = to_core(give)
        return ordered(mine[:, None], theirs[:, None], 1).reshape(bundle, row_count, width)

    def split_far(*parts):
        return mine_of(jnp.concatenate(parts, axis=1), 0)

    def two(part):
        return part.reshape(2, part.shape[0] // 2, own_width)

    def canonical(value):
        if chips == BLOCKS:
            return value
        parts = value.reshape((BLOCKS, chips // BLOCKS) + value.shape[1:])
        return jnp.moveaxis(parts, 1, -2).reshape((BLOCKS,) + value.shape[1:-1] + (wide,))

    def scattered(value):
        if chips == BLOCKS:
            return value
        parts = value.reshape(value.shape[:-1] + (chips // BLOCKS, width // chips))
        return jnp.moveaxis(parts, -2, 1).reshape(
            (chips,) + value.shape[1:-1] + (width // chips,)
        )

    def spread(value, *late):
        return across([value] * narrow, *late)

    near = chips == BLOCKS

    def chips_first(value):
        return (to_chip(value, 1), to_chip(value, 2)) if near else ()

    def chips_second(first, second):
        return to_chip(first[: narrow // 2], 2), to_chip(second[narrow // 2 :], 1)

    def chips_full(value, firsts, seconds):
        if near:
            return jnp.stack([value, *firsts, jnp.concatenate(seconds)])
        return canonical(lax.all_gather(value, "dp", axis_index_groups=same_core))

    def chips_pieces(value, firsts, seconds):
        if near:
            return (value, *firsts, *seconds)
        full = chips_full(value, firsts, seconds)
        return full[0], full[1], full[2], full[3, : narrow // 2], full[3, narrow // 2 :]

    def sum_first(grads):
        x_keep, x_send, y_keep, y_send = grads
        return to_chip(x_send, 1), to_chip(y_send, 2)

    def sum_ready(grads, got):
        x_keep, _, y_keep, _ = grads
        return (
            (x_keep[1].astype(f32) + got[0][1].astype(f32)).astype(bf16),
            (y_keep[1].astype(f32) + got[1][1].astype(f32)).astype(bf16),
        )

    def sum_second(ready):
        return to_chip(ready[0], 2), to_chip(ready[1], 1)

    def sum_done(grads, got, last):
        x_keep, _, y_keep, _ = grads
        x_sum = x_keep[0].astype(f32) + got[0][0].astype(f32) + last[0].astype(f32)
        y_sum = y_keep[0].astype(f32) + got[1][0].astype(f32) + last[1].astype(f32)
        sent = [x_sum[k] for k in range(1, narrow // 2)] + [y_sum[k] for k in range(narrow // 2)]
        return x_sum[0], [block.astype(bf16) for block in sent]

    def sum_far(grads):
        x_keep, x_send, y_keep, y_send = grads
        x_all = jnp.stack([x_keep, x_send], axis=1).reshape((BLOCKS,) + x_keep.shape[1:])
        y_all = jnp.concatenate([y_keep, y_send])
        value = scattered(
            jnp.concatenate([x_all, y_all], axis=1).reshape(BLOCKS, narrow, -1, wide)
        )
        got = lax.psum_scatter(
            value.reshape(-1, value.shape[-1]),
            "dp",
            scatter_dimension=0,
            tiled=True,
            axis_index_groups=same_core,
        ).reshape(value.shape[1:])
        return got[0].astype(f32), [got[k] for k in range(1, narrow)]

    def sum_places(sent, *late):
        got = []
        for k, block in enumerate(sent, 1):
            got.append(along(stage(block, *late) if late and 2 * k == narrow else block, -k))
        return got

    def swap_ready(own, got):
        total = own
        for piece in got:
            total = total + piece.astype(f32)
        low, high = total[:, :own_width], total[:, own_width:]
        return jnp.where(by_core, low, high), jnp.where(by_core, high, low).astype(bf16)

    def finish(keep, theirs, parts, size):
        theirs = theirs.astype(f32)
        both = jnp.where(by_core, jnp.stack([keep, theirs]), jnp.stack([theirs, keep]))
        return [both[:, i * size : (i + 1) * size] for i in range(parts)]

    me = (chip if near else 0 * chip).astype(jnp.int32)[None]
    core_index, place_index = core.astype(jnp.int32)[None], place.astype(jnp.int32)[None]
    kinds = [w_gate.T, w_up.T, w_down]
    depth = w_down.shape[0] // 2
    cut = -(-depth // 32 // 2) * 32
    if near:
        keep, give = square_split_call(
            core_index, bucket, w_query, w_key, w_value, w_out, attn_gain, ffn_gain
        )
    else:
        extra = jnp.concatenate(
            [
                attn_gain[None],
                ffn_gain[None],
                jnp.pad(bucket.astype(bf16), (0, own_width - bundle))[None],
                jnp.zeros((13, own_width), bf16),
            ]
        )
        keep, give = split_far(
            two(w_query.T), two(w_key.T), two(w_value.T), two(w_out), jnp.stack([extra, extra])
        )
        halves = [two(kind) for kind in kinds]
        ffn_keep, ffn_give = split_far(
            *[half[:, :cut] for half in halves], *[half[:, cut:] for half in halves]
        )
    square = ordered(keep, to_core(give), 1)

    square_z = spread(square)
    own_inputs, own_cotangent, kinds, square = stage((inputs, cotangent, kinds, square))
    if near:
        ffn_keep, ffn_give = ffn_split_call(core_index, cut, *kinds)
    x_blocks = blocks_for(group_start(own_inputs))
    cot_blocks = blocks_for(group_start(own_cotangent))
    ffn_theirs = to_core(ffn_give)
    ffn_one = ordered(ffn_keep[: 3 * cut], ffn_theirs[: 3 * cut], 1)
    ffn_two = ordered(ffn_keep[3 * cut :], ffn_theirs[3 * cut :], 1)
    flags = square[4 * 128 + 2].reshape(2, own_width)[:, :bundle].reshape(-1)
    flag = pick(flags.astype(jnp.int32), place, 0)[None]

    square_z, x_blocks, cot_blocks, ffn_one, ffn_two, flag = stage(
        (square_z, x_blocks, cot_blocks, ffn_one, ffn_two, flag)
    )
    square_z = jnp.stack(square_z)
    square_first = chips_first(square_z)
    x_moved = across(x_blocks)

    square_first, x_moved, ffn_one = stage((square_first, x_moved, ffn_one))
    x_own = jnp.stack(x_moved)
    x_other = to_core(x_own)
    square_second = chips_second(*square_first) if near else ()
    one_z = spread(ffn_one, x_other)
    square_full = chips_full(square_z, square_first, square_second)
    x_rows, hidden, rms, gains, q, k, v = qkv_call(
        me, core_index, place_index, x_own, x_other, square_full
    )

    q, one_z, cot_blocks = stage((q, one_z, cot_blocks))
    one_z = jnp.stack(one_z)
    one_first = chips_first(one_z)
    cot_moved = across(cot_blocks)
    attended, probs = attend_call(flag, q, k, v)

    attended, one_first, cot_moved, ffn_two = stage((attended, one_first, cot_moved, ffn_two))
    one_second = chips_second(*one_first) if near else ()
    branch = branch_call(me, attended, square_full)
    cot_own = jnp.stack(cot_moved)
    two_z = spread(ffn_two, branch)
    middle_place = narrow // 2
    branch, cot_own, one_second, two_near = stage(
        (branch, cot_own, one_second, two_z[:middle_place] + two_z[middle_place + 1 :])
    )
    two_z = two_near[:middle_place] + [two_z[middle_place]] + two_near[middle_place:]
    branch_other, cot_other = to_core(branch), to_core(cot_own)
    middle, normed, cot_rows = middle_call(
        core_index, place_index, x_rows, branch, branch_other, gains, cot_own, cot_other
    )

    normed, two_z = stage((normed, two_z))
    two_z = jnp.stack(two_z)
    two_first = chips_first(two_z)
    part_result, part_d_normed, *one_grads = ffn_call(
        me, normed, cot_rows, chips_pieces(one_z, one_first, one_second)
    )

    part_result, part_d_normed, one_grads, two_first = stage(
        (part_result, part_d_normed, one_grads, two_first)
    )
    two_second = chips_second(*two_first) if near else ()

    part_result, part_d_normed, one_grads, two_second = stage(
        (part_result, part_d_normed, one_grads, two_second)
    )
    one_got = sum_first(one_grads) if near else ()
    result, d_normed, *two_grads = ffn_call(
        me,
        normed,
        cot_rows,
        chips_pieces(two_z, two_first, two_second),
        part_result,
        part_d_normed,
    )

    result, d_normed, two_grads, one_got = stage((result, d_normed, two_grads, one_got))
    by_rows = (narrow, 2, tile, width)
    d_normed_other = to_core(d_normed)
    one_last = sum_second(sum_ready(one_grads, one_got)) if near else ()
    result = result.reshape(by_rows)
    result_other = to_core(mine_of(result, 1)[1])
    d_middle, d_branch, d_att, ffn_gain_grad, out_rows = turn_call(
        me,
        core_index,
        middle,
        d_normed,
        d_normed_other,
        cot_rows,
        gains,
        square_full,
        result,
        result_other,
    )
    out_blocks = blocks_for(out_rows)

    d_att, out_blocks, one_last, two_grads = stage((d_att, out_blocks, one_last, two_grads))
    two_got = sum_first(two_grads) if near else ()
    out_moved = across(out_blocks)
    dq, dk, dv = attend_back_call(flag, q, k, v, attended, d_att, probs)
    one_own, one_sent = sum_done(one_grads, one_got, one_last) if near else sum_far(one_grads)

    dq, one_sent, two_got, out_moved = stage((dq, one_sent, two_got, out_moved))
    two_last = sum_second(sum_ready(two_grads, two_got)) if near else ()
    one_places = sum_places(one_sent)
    d_hidden, *square_grads = square_call(
        me, dq, dk, dv, attended, hidden, d_branch, square_full, x_rows, rms, 0.5 * ffn_gain_grad
    )
    outputs = group_back(out_moved)

    d_hidden, square_grads, two_last, one_places = stage(
        (d_hidden, square_grads, two_last, one_places)
    )
    square_got = sum_first(square_grads) if near else ()
    d_hidden = d_hidden.reshape(by_rows)
    d_hidden_other = to_core(mine_of(d_hidden, 1)[1])
    two_own, two_sent = sum_done(two_grads, two_got, two_last) if near else sum_far(two_grads)
    two_places = sum_places(two_sent, d_hidden_other)
    input_blocks = blocks_for(
        input_call(core_index, x_rows, d_middle, d_hidden, d_hidden_other, gains)
    )
    one_keep, one_swap = swap_ready(one_own, one_places)

    input_blocks, square_got, two_places, one_swap = stage(
        (input_blocks, square_got, two_places, one_swap)
    )
    square_last = sum_second(sum_ready(square_grads, square_got)) if near else ()
    input_moved = across(input_blocks)
    one_theirs = to_core(one_swap)
    two_keep, two_swap = swap_ready(two_own, two_places)
    two_theirs = to_core(two_swap)

    square_last, input_moved, one_theirs, two_theirs = stage(
        (square_last, input_moved, one_theirs, two_theirs)
    )
    square_own, square_sent = (
        sum_done(square_grads, square_got, square_last) if near else sum_far(square_grads)
    )
    square_places = sum_places(square_sent)
    input_grad = group_back(input_moved).astype(f32)
    one_parts = finish(one_keep, one_theirs, 3, cut)
    two_parts = finish(two_keep, two_theirs, 3, depth - cut)
    g_gate, g_up, g_down = [
        jnp.concatenate(parts, axis=1).reshape(2 * depth, own_width)
        for parts in zip(one_parts, two_parts)
    ]
    g_gate, g_up = g_gate.T, g_up.T
    square_places, outputs, input_grad, g_gate, g_up, g_down = stage(
        (square_places, outputs, input_grad, g_gate, g_up, g_down)
    )
    square_keep, square_swap = swap_ready(square_own, square_places)
    square_theirs = to_core(square_swap)
    g_query, g_key, g_value, g_out = [
        part.reshape(-1, own_width) for part in finish(square_keep, square_theirs, 4, 128)
    ]
    gain_own = square_keep[4 * 128 :] + square_theirs[4 * 128 :].astype(f32)
    return (
        outputs,
        input_grad,
        gain_own[0],
        g_query.T,
        g_key.T,
        g_value.T,
        g_out,
        gain_own[1],
        g_gate,
        g_up,
        g_down,
    )


def solution(mesh):
    rows = P("dp", "narrow", None)
    tall, flat = P("dp", "narrow"), P("narrow", "dp")
    return jax.shard_map(
        per_device,
        mesh=mesh,
        in_specs=(rows, P("dp"), P("dp"), tall, tall, tall, flat, P("dp"), tall, tall, flat, rows),
        out_specs=(rows, rows, P("dp"), tall, tall, tall, flat, P("dp"), tall, tall, flat),
        check_vma=False,
    )
```

profile of v0, /device:TPU:0, one launch (start us, length us, event | category | flops | bytes accessed | tf_op | source)
XLA Modules:
  0.0 419.8 jit_solution(6322387475599187659)
XLA Ops:
  28.1 3.8 collective-permute-done.2
  38.2 4.1 collective-permute-start.9
  44.7 6.8 %collective-permute-done.9 = bf16[144,1024]{1,0:T(8,128)(2,1)S(1)} collective-permute-done((bf16[144,1024]{1,0:T(8,128)(2,1)S(1)}, bf16[144,1024]{1,0:T(8,128)(2,1)S(1)}, u32[]{:S(2)}, u32[]{:S(2)}) %collective-permute-start.9) | collective-permute-done | bytes 294944 | tf_op jit(solution)/shard_map/ppermute | solution.py:702
  51.5 10.6 %collective-permute-done.10 = bf16[144,1024]{1,0:T(8,128)(2,1)S(1)} collective-permute-done((bf16[144,1024]{1,0:T(8,128)(2,1)S(1)}, bf16[144,1024]{1,0:T(8,128)(2,1)S(1)}, u32[]{:S(2)}, u32[]{:S(2)}) %collective-permute-start.10) | collective-permute-done | bytes 294944 | tf_op jit(solution)/shard_map/ppermute | solution.py:702
  66.2 6.5 %collective-permute-start.15 = (bf16[576,256]{1,0:T(8,128)(2,1)}, bf16[576,256]{1,0:T(8,128)(2,1)S(1)}, u32[]{:S(2)}, u32[]{:S(2)}) collective-permute-start(bf16[576,256]{1,0:T(8,128)(2,1)} %maximum_select_fusion.11), channel_id=1, source_target_pairs={{0,1},{1,2},{2,3},{3,0},{4,5},{5,6},{6,7},{7,4},{8,9},{9,10},{10,1... | collective-permute-start | bytes 884744 | tf_op jit(solution)/shard_map/ppermute | solution.py:702
  74.1 4.4 %collective-permute-done.14 = bf16[2,528,256]{2,1,0:T(8,128)(2,1)} collective-permute-done((bf16[2,528,256]{2,1,0:T(8,128)(2,1)}, bf16[2,528,256]{2,1,0:T(8,128)(2,1)}, u32[]{:S(2)}, u32[]{:S(2)}) %collective-permute-start.14) | collective-permute-done | bytes 540704 | tf_op jit(solution)/shard_map/ppermute | solution.py:699
  84.3 5.8 %collective-permute-start.16 = (bf16[576,256]{1,0:T(8,128)(2,1)S(1)}, bf16[576,256]{1,0:T(8,128)(2,1)S(1)}, u32[]{:S(2)}, u32[]{:S(2)}) collective-permute-start(bf16[576,256]{1,0:T(8,128)(2,1)S(1)} %copy-done.41), channel_id=1, source_target_pairs={{0,2},{1,3},{2,0},{3,1},{4,6},{5,7},{6,4},{7,5},{8,10},{9,11},{10,... | collective-permute-start | bytes 884744 | tf_op jit(solution)/shard_map/ppermute | solution.py:702
  91.4 8.2 %shard_map.205 = (bf16[1152,1024]{1,0:T(8,128)(2,1)S(1)}, bf16[1152,1024]{1,0:T(8,128)(2,1)S(1)}, f32[1152,128]{1,0:T(8,128)S(1)}, f32[8,1024]{1,0:T(8,128)S(1)}...) custom-call(s32[1]{0:T(128)} %bitcast.me_ref, s32[1]{0:T(128)} %bitcast.1.core_ref, ...), custom_call_target="tpu_custom_call" | custom-call | flops 3623878656 | bytes 12582912 | tf_op jit(solution)/shard_map/pallas_call | solution.py:198
  113.7 24.9 %shard_map.206 = (bf16[1152,512]{1,0:T(8,128)(2,1)S(1)}, bf16[4,3,1152,768]{3,2,1,0:T(8,128)(2,1)}) custom-call(s32[1]{0:T(128)} %dynamic_slice.85.flag_ref, bf16[1152,512]{1,0:T(8,128)(2,1)S(1)} %copy-done.29, bf16[1152,512]{1,0:T(8,128)(2,1)S(1)} %copy-done.32, bf16[1152,512]{1,0:T(8,128)(2,1)S(1)} %get-tuple-element.228.v_ref), custom_call_target="tpu_custom_call" | custom-call | flops 10871635968 | bytes 29360128 | tf_op jit(solution)/shard_map/pallas_call | solution.py:268
  143.0 3.0 collective-permute-start.26
  154.8 4.6 %collective-permute-done.28.other_ref = bf16[4,144,1024]{2,1,0:T(8,128)(2,1)S(1)} collective-permute-done((bf16[4,144,1024]{2,1,0:T(8,128)(2,1)S(1)}, bf16[4,144,1024]{2,1,0:T(8,128)(2,1)S(1)}, u32[]{:S(2)}, u32[]{:S(2)}) %collective-permute-start.28) | collective-permute-done | bytes 1179680 | tf_op jit(solution)/shard_map/ppermute | solution.py:696
  170.3 24.2 %shard_map.209 = (bf16[1152,1024]{1,0:T(8,128)(2,1)}, bf16[1152,1024]{1,0:T(8,128)(2,1)}, bf16[2,2,576,256]{3,2,1,0:T(8,128)(2,1)}, bf16[2,2,576,256]{3,2,1,0:T(...) custom-call(s32[1]{0:T(128)} %bitcast.me_ref, bf16[1152,1024]{1,0:T(8,128)(2,1)} %copy-done.22, ...), custom_call_target="tpu_custom_call" | custom-call | flops 16307453952 | bytes 20971520 | tf_op jit(solution)/shard_map/pallas_call | solution.py:408
  196.4 10.5 %collective-permute-done.32.refs_3_ = bf16[2,480,256]{2,1,0:T(8,128)(2,1)S(1)} collective-permute-done((bf16[2,480,256]{2,1,0:T(8,128)(2,1)S(1)}, bf16[2,480,256]{2,1,0:T(8,128)(2,1)S(1)}, u32[]{:S(2)}, u32[]{:S(2)}) %collective-permute-start.32) | collective-permute-done | bytes 491552 | tf_op jit(solution)/shard_map/ppermute | solution.py:699
  209.2 25.5 %shard_map.210 = (bf16[1152,1024]{1,0:T(8,128)(2,1)}, bf16[1152,1024]{1,0:T(8,128)(2,1)}, bf16[2,2,480,256]{3,2,1,0:T(8,128)(2,1)}, bf16[2,2,480,256]{3,2,1,0:T(...) custom-call(s32[1]{0:T(128)} %bitcast.me_ref, bf16[1152,1024]{1,0:T(8,128)(2,1)} %copy-done.22, ...), custom_call_target="tpu_custom_call" | custom-call | flops 13589544960 | bytes 20971520 | tf_op jit(solution)/shard_map/pallas_call | solution.py:408
  234.8 3.6 fusion.3
  245.4 8.0 %shard_map.211 = (f32[1152,1024]{1,0:T(8,128)}, bf16[1152,1024]{1,0:T(8,128)(2,1)S(1)}, bf16[1152,512]{1,0:T(8,128)(2,1)S(1)}, f32[1,1024]{1,0:T(1,128)S(1)}, bf16[4,144,1024]{2,1,0:T(8,128)(2,1)S(1)}) custom-call(s32[1]{0:T(128)} %bitcast.me_ref, s32[1]{0:T(128)} %bitcast.1.core_ref, f32[1152,1024]{1,0:T(8,128)} %copy-done.2, ...), custom_call_target="tpu_custom_call" | custom-call | flops 1207959552 | bytes 23068672 | tf_op jit(solution)/shard_map/pallas_call | solution.py:479
  265.1 30.0 %shard_map.212 = (bf16[1152,512]{1,0:T(8,128)(2,1)S(1)}, bf16[1152,512]{1,0:T(8,128)(2,1)S(1)}, bf16[1152,512]{1,0:T(8,128)(2,1)S(1)}) custom-call(s32[1]{0:T(128)} %dynamic_slice.85.flag_ref, bf16[1152,512]{1,0:T(8,128)(2,1)S(1)} %copy-done.30, bf16[1152,512]{1,0:T(8,128)(2,1)S(1)} %copy-done.33, bf16[1152,512]{1,0:T(8,128)(2,1)} %copy-done.34, ...), custom_call_target="tpu_custom_call" | custom-call | flops 21743271936 | bytes 31457280 | tf_op jit(solution)/shard_map/pallas_call | solution.py:560
  305.4 19.8 %shard_map.213 = (bf16[1152,1024]{1,0:T(8,128)(2,1)S(1)}, bf16[2,2,528,256]{3,2,1,0:T(8,128)(2,1)S(1)}, bf16[2,2,528,256]{3,2,1,0:T(8,128)(2,1)S(1)}, bf16[2,2,5...) custom-call(s32[1]{0:T(128)} %bitcast.me_ref, bf16[1152,512]{1,0:T(8,128)(2,1)S(1)} %get-tuple-element.314.dq_ref, ...), custom_call_target="tpu_custom_call" | custom-call | flops 8455716864 | bytes 25165824 | tf_op jit(solution)/shard_map/pallas_call | solution.py:623
  337.9 7.2 %collective-permute-done.55 = bf16[480,256]{1,0:T(8,128)(2,1)S(1)} collective-permute-done((bf16[480,256]{1,0:T(8,128)(2,1)S(1)}, bf16[480,256]{1,0:T(8,128)(2,1)S(1)}, u32[]{:S(2)}, u32[]{:S(2)}) %collective-permute-start.55) | collective-permute-done | bytes 245792 | tf_op jit(solution)/shard_map/ppermute | solution.py:702
  345.1 9.1 %collective-permute-done.51 = bf16[2,2,528,256]{3,2,1,0:T(8,128)(2,1)S(1)} collective-permute-done((bf16[2,2,528,256]{3,2,1,0:T(8,128)(2,1)S(1)}, bf16[2,2,528,256]{3,2,1,0:T(8,128)(2,1)S(1)}, u32[]{:S(2)}, u32[]{:S(2)}) %collective-permute-start.51) | collective-permute-done | bytes 1081376 | tf_op jit(solution)/shard_map/ppermute | solution.py:699
  362.9 7.2 %collective-permute-done.58 = bf16[144,1024]{1,0:T(8,128)(2,1)S(1)} collective-permute-done((bf16[144,1024]{1,0:T(8,128)(2,1)S(1)}, bf16[144,1024]{1,0:T(8,128)(2,1)S(1)}, u32[]{:S(2)}, u32[]{:S(2)}) %collective-permute-start.58) | collective-permute-done | bytes 294944 | tf_op jit(solution)/shard_map/ppermute | solution.py:702
  370.1 11.7 %collective-permute-done.59 = bf16[144,1024]{1,0:T(8,128)(2,1)S(1)} collective-permute-done((bf16[144,1024]{1,0:T(8,128)(2,1)S(1)}, bf16[144,1024]{1,0:T(8,128)(2,1)S(1)}, u32[]{:S(2)}, u32[]{:S(2)}) %collective-permute-start.59) | collective-permute-done | bytes 294944 | tf_op jit(solution)/shard_map/ppermute | solution.py:702
  382.0 7.0 %collective-permute-start.63 = (bf16[528,256]{1,0:T(8,128)(2,1)S(1)}, bf16[528,256]{1,0:T(8,128)(2,1)S(1)}, u32[]{:S(2)}, u32[]{:S(2)}) collective-permute-start(bf16[528,256]{1,0:T(8,128)(2,1)S(1)} %fusion.23), channel_id=1, source_target_pairs={{0,3},{1,0},{2,1},{3,2},{4,7},{5,4},{6,5},{7,6},{8,11},{9,8},{10,9... | collective-permute-start | bytes 811016 | tf_op jit(solution)/shard_map/ppermute | solution.py:702
  398.0 16.2 %collective-permute-done.64 = bf16[528,256]{1,0:T(8,128)(2,1)S(1)} collective-permute-done((bf16[528,256]{1,0:T(8,128)(2,1)S(1)}, bf16[528,256]{1,0:T(8,128)(2,1)S(1)}, u32[]{:S(2)}, u32[]{:S(2)}) %collective-permute-start.64) | collective-permute-done | bytes 270368 | tf_op jit(solution)/shard_map/ppermute | solution.py:702
  (375 shorter events, 154.5 us)
Async XLA Ops:
  35.1 27.1 %collective-permute-start.7 = (bf16[4,528,256]{2,1,0:T(8,128)(2,1)S(1)}, bf16[4,528,256]{2,1,0:T(8,128)(2,1)S(1)}, u32[]{:S(2)}, u32[]{:S(2)}) collective-permute-start(bf16[4,528,256]{2,1,0:T(8,128)(2,1)S(1)} %get-tuple-element.404), channel_id=1, source_target_pairs={{0,8},{4,12},{8,0},{12,4},{16,24},{20,28},{24,16},{28,20},{1,9},{5... | collective-permute-start | bytes 3244040 | tf_op jit(solution)/shard_map/ppermute | solution.py:699
  36.7 25.5 %collective-permute-start.8 = (bf16[4,528,256]{2,1,0:T(8,128)(2,1)S(1)}, bf16[4,528,256]{2,1,0:T(8,128)(2,1)S(1)}, u32[]{:S(2)}, u32[]{:S(2)}) collective-permute-start(bf16[4,528,256]{2,1,0:T(8,128)(2,1)S(1)} %get-tuple-element.404), channel_id=1, source_target_pairs={{0,16},{4,20},{8,24},{12,28},{16,0},{20,4},{24,8},{28,12},{1,17},{... | collective-permute-start | bytes 3244040 | tf_op jit(solution)/shard_map/ppermute | solution.py:699
  66.2 37.7 %collective-permute-start.15 = (bf16[576,256]{1,0:T(8,128)(2,1)}, bf16[576,256]{1,0:T(8,128)(2,1)S(1)}, u32[]{:S(2)}, u32[]{:S(2)}) collective-permute-start(bf16[576,256]{1,0:T(8,128)(2,1)} %maximum_select_fusion.11), channel_id=1, source_target_pairs={{0,1},{1,2},{2,3},{3,0},{4,5},{5,6},{6,7},{7,4},{8,9},{9,10},{10,1... | collective-permute-start | bytes 884744 | tf_op jit(solution)/shard_map/ppermute | solution.py:702
  72.7 31.2 %collective-permute-start.17 = (bf16[576,256]{1,0:T(8,128)(2,1)}, bf16[576,256]{1,0:T(8,128)(2,1)S(1)}, u32[]{:S(2)}, u32[]{:S(2)}) collective-permute-start(bf16[576,256]{1,0:T(8,128)(2,1)} %maximum_select_fusion.11), channel_id=1, source_target_pairs={{0,3},{1,0},{2,1},{3,2},{4,7},{5,4},{6,5},{7,6},{8,11},{9,8},{10,9... | collective-permute-start | bytes 884744 | tf_op jit(solution)/shard_map/ppermute | solution.py:702
  104.1 35.6 %collective-permute-start.18 = (bf16[4,576,256]{2,1,0:T(8,128)(2,1)S(1)}, bf16[4,576,256]{2,1,0:T(8,128)(2,1)S(1)}, u32[]{:S(2)}, u32[]{:S(2)}) collective-permute-start(bf16[4,576,256]{2,1,0:T(8,128)(2,1)S(1)} %pad_maximum_fusion.2.refs_0_), channel_id=1, source_target_pairs={{0,8},{4,12},{8,0},{12,4},{16,24},{20,28},{24,16},{28,20},{1,9},{5... | collective-permute-start | bytes 3538952 | tf_op jit(solution)/shard_map/ppermute | solution.py:699
  105.7 34.0 %collective-permute-start.19 = (bf16[4,576,256]{2,1,0:T(8,128)(2,1)S(1)}, bf16[4,576,256]{2,1,0:T(8,128)(2,1)S(1)}, u32[]{:S(2)}, u32[]{:S(2)}) collective-permute-start(bf16[4,576,256]{2,1,0:T(8,128)(2,1)S(1)} %pad_maximum_fusion.2.refs_0_), channel_id=1, source_target_pairs={{0,16},{4,20},{8,24},{12,28},{16,0},{20,4},{24,8},{28,12},{1,17},{... | collective-permute-start | bytes 3538952 | tf_op jit(solution)/shard_map/ppermute | solution.py:699
  106.2 33.5 %collective-permute-start.20 = (bf16[144,1024]{1,0:T(8,128)(2,1)}, bf16[144,1024]{1,0:T(8,128)(2,1)S(1)}, u32[]{:S(2)}, u32[]{:S(2)}) collective-permute-start(bf16[144,1024]{1,0:T(8,128)(2,1)} %get-tuple-element.235), channel_id=1, source_target_pairs={{0,1},{1,2},{2,3},{3,0},{4,5},{5,6},{6,7},{7,4},{8,9},{9,10},{10,1... | collective-permute-start | bytes 884744 | tf_op jit(solution)/shard_map/ppermute | solution.py:702
  108.8 30.9 %collective-permute-start.21 = (bf16[144,1024]{1,0:T(8,128)(2,1)S(1)}, bf16[144,1024]{1,0:T(8,128)(2,1)S(1)}, u32[]{:S(2)}, u32[]{:S(2)}) collective-permute-start(bf16[144,1024]{1,0:T(8,128)(2,1)S(1)} %copy-done.66), channel_id=1, source_target_pairs={{0,2},{1,3},{2,0},{3,1},{4,6},{5,7},{6,4},{7,5},{8,10},{9,11},{10,... | collective-permute-start | bytes 884744 | tf_op jit(solution)/shard_map/ppermute | solution.py:702
  110.1 29.6 %collective-permute-start.22 = (bf16[144,1024]{1,0:T(8,128)(2,1)S(1)}, bf16[144,1024]{1,0:T(8,128)(2,1)S(1)}, u32[]{:S(2)}, u32[]{:S(2)}) collective-permute-start(bf16[144,1024]{1,0:T(8,128)(2,1)S(1)} %copy-done.65), channel_id=1, source_target_pairs={{0,3},{1,0},{2,1},{3,2},{4,7},{5,4},{6,5},{7,6},{8,11},{9,8},{10,9... | collective-permute-start | bytes 884744 | tf_op jit(solution)/shard_map/ppermute | solution.py:702
  167.8 26.6 %collective-permute-start.30 = (bf16[4,480,256]{2,1,0:T(8,128)(2,1)S(1)}, bf16[4,480,256]{2,1,0:T(8,128)(2,1)S(1)}, u32[]{:S(2)}, u32[]{:S(2)}) collective-permute-start(bf16[4,480,256]{2,1,0:T(8,128)(2,1)S(1)} %pad_maximum_fusion.8.refs_0_), channel_id=1, source_target_pairs={{0,8},{4,12},{8,0},{12,4},{16,24},{20,28},{24,16},{28,20},{1,9},{5... | collective-permute-start | bytes 2949128 | tf_op jit(solution)/shard_map/ppermute | solution.py:699
  169.2 25.3 %collective-permute-start.31 = (bf16[4,480,256]{2,1,0:T(8,128)(2,1)S(1)}, bf16[4,480,256]{2,1,0:T(8,128)(2,1)S(1)}, u32[]{:S(2)}, u32[]{:S(2)}) collective-permute-start(bf16[4,480,256]{2,1,0:T(8,128)(2,1)S(1)} %pad_maximum_fusion.8.refs_0_), channel_id=1, source_target_pairs={{0,16},{4,20},{8,24},{12,28},{16,0},{20,4},{24,8},{28,12},{1,17},{... | collective-permute-start | bytes 2949128 | tf_op jit(solution)/shard_map/ppermute | solution.py:699
  207.7 27.0 %collective-permute-start.34 = (bf16[2,2,576,256]{3,2,1,0:T(8,128)(2,1)}, bf16[2,2,576,256]{3,2,1,0:T(8,128)(2,1)S(1)}, u32[]{:S(2)}, u32[]{:S(2)}) collective-permute-start(bf16[2,2,576,256]{3,2,1,0:T(8,128)(2,1)} %get-tuple-element.289), channel_id=1, source_target_pairs={{0,8},{4,12},{8,0},{12,4},{16,24},{20,28},{24,16},{28,20},{1,9},{5... | collective-permute-start | bytes 3538952 | tf_op jit(solution)/shard_map/ppermute | solution.py:699
  208.0 26.7 %collective-permute-start.35 = (bf16[2,2,576,256]{3,2,1,0:T(8,128)(2,1)S(1)}, bf16[2,2,576,256]{3,2,1,0:T(8,128)(2,1)S(1)}, u32[]{:S(2)}, u32[]{:S(2)}) collective-permute-start(bf16[2,2,576,256]{3,2,1,0:T(8,128)(2,1)S(1)} %copy-done.69), channel_id=1, source_target_pairs={{0,16},{4,20},{8,24},{12,28},{16,0},{20,4},{24,8},{28,12},{1,17},{... | collective-permute-start | bytes 3538952 | tf_op jit(solution)/shard_map/ppermute | solution.py:699
  258.5 39.2 %collective-permute-start.40 = (bf16[2,2,480,256]{3,2,1,0:T(8,128)(2,1)}, bf16[2,2,480,256]{3,2,1,0:T(8,128)(2,1)S(1)}, u32[]{:S(2)}, u32[]{:S(2)}) collective-permute-start(bf16[2,2,480,256]{3,2,1,0:T(8,128)(2,1)} %get-tuple-element.308), channel_id=1, source_target_pairs={{0,8},{4,12},{8,0},{12,4},{16,24},{20,28},{24,16},{28,20},{1,9},{5... | collective-permute-start | bytes 2949128 | tf_op jit(solution)/shard_map/ppermute | solution.py:699
  260.2 37.5 %collective-permute-start.41 = (bf16[2,2,480,256]{3,2,1,0:T(8,128)(2,1)}, bf16[2,2,480,256]{3,2,1,0:T(8,128)(2,1)}, u32[]{:S(2)}, u32[]{:S(2)}) collective-permute-start(bf16[2,2,480,256]{3,2,1,0:T(8,128)(2,1)} %get-tuple-element.309), channel_id=1, source_target_pairs={{0,16},{4,20},{8,24},{12,28},{16,0},{20,4},{24,8},{28,12},{1,17},{... | collective-permute-start | bytes 2949128 | tf_op jit(solution)/shard_map/ppermute | solution.py:699
  261.3 36.3 %collective-permute-start.42 = (bf16[144,1024]{1,0:T(8,128)(2,1)}, bf16[144,1024]{1,0:T(8,128)(2,1)S(1)}, u32[]{:S(2)}, u32[]{:S(2)}) collective-permute-start(bf16[144,1024]{1,0:T(8,128)(2,1)} %get-tuple-element.311), channel_id=1, source_target_pairs={{0,1},{1,2},{2,3},{3,0},{4,5},{5,6},{6,7},{7,4},{8,9},{9,10},{10,1... | collective-permute-start | bytes 884744 | tf_op jit(solution)/shard_map/ppermute | solution.py:702
  261.3 36.3 %collective-permute-start.43 = (bf16[144,1024]{1,0:T(8,128)(2,1)S(1)}, bf16[144,1024]{1,0:T(8,128)(2,1)S(1)}, u32[]{:S(2)}, u32[]{:S(2)}) collective-permute-start(bf16[144,1024]{1,0:T(8,128)(2,1)S(1)} %get-tuple-element.312), channel_id=1, source_target_pairs={{0,2},{1,3},{2,0},{3,1},{4,6},{5,7},{6,4},{7,5},{8,10},{9,11},{10,... | collective-permute-start | bytes 884744 | tf_op jit(solution)/shard_map/ppermute | solution.py:702
  263.9 33.7 %collective-permute-start.44 = (bf16[144,1024]{1,0:T(8,128)(2,1)S(1)}, bf16[144,1024]{1,0:T(8,128)(2,1)S(1)}, u32[]{:S(2)}, u32[]{:S(2)}) collective-permute-start(bf16[144,1024]{1,0:T(8,128)(2,1)S(1)} %get-tuple-element.313), channel_id=1, source_target_pairs={{0,3},{1,0},{2,1},{3,2},{4,7},{5,4},{6,5},{7,6},{8,11},{9,8},{10,9... | collective-permute-start | bytes 884744 | tf_op jit(solution)/shard_map/ppermute | solution.py:702
  297.8 29.8 %collective-permute-start.45 = (bf16[2,480,256]{2,1,0:T(8,128)(2,1)S(1)}, bf16[2,480,256]{2,1,0:T(8,128)(2,1)S(1)}, u32[]{:S(2)}, u32[]{:S(2)}) collective-permute-start(bf16[2,480,256]{2,1,0:T(8,128)(2,1)S(1)} %fusion.17), channel_id=1, source_target_pairs={{0,16},{4,20},{8,24},{12,28},{16,0},{20,4},{24,8},{28,12},{1,17},{... | collective-permute-start | bytes 1474568 | tf_op jit(solution)/shard_map/ppermute | solution.py:699
  300.3 27.4 %collective-permute-start.46 = (bf16[2,480,256]{2,1,0:T(8,128)(2,1)}, bf16[2,480,256]{2,1,0:T(8,128)(2,1)}, u32[]{:S(2)}, u32[]{:S(2)}) collective-permute-start(bf16[2,480,256]{2,1,0:T(8,128)(2,1)} %fusion.18), channel_id=1, source_target_pairs={{0,8},{4,12},{8,0},{12,4},{16,24},{20,28},{24,16},{28,20},{1,9},{5... | collective-permute-start | bytes 1474568 | tf_op jit(solution)/shard_map/ppermute | solution.py:699
  327.9 26.3 %collective-permute-start.51 = (bf16[2,2,528,256]{3,2,1,0:T(8,128)(2,1)S(1)}, bf16[2,2,528,256]{3,2,1,0:T(8,128)(2,1)S(1)}, u32[]{:S(2)}, u32[]{:S(2)}) collective-permute-start(bf16[2,2,528,256]{3,2,1,0:T(8,128)(2,1)S(1)} %get-tuple-element.336), channel_id=1, source_target_pairs={{0,8},{4,12},{8,0},{12,4},{16,24},{20,28},{24,16},{28,20},{1,9},{5... | collective-permute-start | bytes 3244040 | tf_op jit(solution)/shard_map/ppermute | solution.py:699
  329.1 25.9 %collective-permute-start.52 = (bf16[2,2,528,256]{3,2,1,0:T(8,128)(2,1)S(1)}, bf16[2,2,528,256]{3,2,1,0:T(8,128)(2,1)S(1)}, u32[]{:S(2)}, u32[]{:S(2)}) collective-permute-start(bf16[2,2,528,256]{3,2,1,0:T(8,128)(2,1)S(1)} %get-tuple-element.337), channel_id=1, source_target_pairs={{0,16},{4,20},{8,24},{12,28},{16,0},{20,4},{24,8},{28,12},{1,17},{... | collective-permute-start | bytes 3244040 | tf_op jit(solution)/shard_map/ppermute | solution.py:699
  355.2 26.6 %collective-permute-start.56 = (bf16[2,528,256]{2,1,0:T(8,128)(2,1)S(1)}, bf16[2,528,256]{2,1,0:T(8,128)(2,1)S(1)}, u32[]{:S(2)}, u32[]{:S(2)}) collective-permute-start(bf16[2,528,256]{2,1,0:T(8,128)(2,1)S(1)} %fusion.12), channel_id=1, source_target_pairs={{0,16},{4,20},{8,24},{12,28},{16,0},{20,4},{24,8},{28,12},{1,17},{... | collective-permute-start | bytes 1622024 | tf_op jit(solution)/shard_map/ppermute | solution.py:699
  356.0 25.8 %collective-permute-start.57 = (bf16[2,528,256]{2,1,0:T(8,128)(2,1)S(1)}, bf16[2,528,256]{2,1,0:T(8,128)(2,1)S(1)}, u32[]{:S(2)}, u32[]{:S(2)}) collective-permute-start(bf16[2,528,256]{2,1,0:T(8,128)(2,1)S(1)} %fusion.13), channel_id=1, source_target_pairs={{0,8},{4,12},{8,0},{12,4},{16,24},{20,28},{24,16},{28,20},{1,9},{5... | collective-permute-start | bytes 1622024 | tf_op jit(solution)/shard_map/ppermute | solution.py:699
  (123 other events, 1257.8 us)
where the time goes:
time: 427 us; the launch traced here: 420 us
  Pallas kernels  147 us (34%)
  waiting for transfers between devices  110 us (26%)
  starting transfers between devices  88.9 us (21%)
  local copies, waits for them, and re-layouts  40.6 us (10%)
  other arithmetic  31.7 us (7%)
    ppermute x30, waiting for transfers between devices, along(): lax.ppermute(value, 'narrow', [(i, (i + shift) % narrow) for i in range(n...  73.8 us
    ppermute x30, starting transfers between devices, along(): lax.ppermute(value, 'narrow', [(i, (i + shift) % narrow) for i in range(n...  61.5 us
    pallas_call x2, Pallas kernels, ffn_call(): call(functools.partial(ffn_kernel, len(weights), bool(before)), (), 1, [w...  49.7 us
    pallas_call x1, Pallas kernels, attend_back_call(): call(attend_back_kernel, (pairs, blocks), 1, [some, every, every, some, s...  30 us
    ppermute x24, waiting for transfers between devices, to_chip(): return lax.ppermute(value, 'dp', [(i, i ^ 2 * flip) for i in range(dp)])  28.1 us
    unnamed x156, local copies, waits for them, and re-layouts  27 us
    pallas_call x1, Pallas kernels, attend_call(): call(attend_kernel, (pairs, blocks), 1, [some, every, every], [some, pl.B...  24.9 us
    ppermute x24, starting transfers between devices, to_chip(): return lax.ppermute(value, 'dp', [(i, i ^ 2 * flip) for i in range(dp)])  23.8 us
  transfers between devices with their start and end apart: 69, of which 24 were waited for; matrix products, arithmetic and copies ran while one was open for 9% of the time, Pallas kernels for 35%

commit v1 on v0

--- a/solution.py
+++ b/solution.py
@@ -161,8 +161,15 @@
 
 
 def qkv_kernel(
-    me_ref, core_ref, place_ref, own_ref, other_ref, w_ref, x_ref, hidden_ref, rms_ref, gains_ref, q_ref, k_ref, v_ref
+    me_ref, core_ref, place_ref, own_ref, other_ref, w0, w1, w2, w3, w4, x_ref, hidden_ref, rms_ref, gains_ref, w_ref, q_ref, k_ref, v_ref
 ):
+    @pl.when(pl.program_id(0) == 0)
+    def _():
+        for step, piece in enumerate((w0, w1, w2)):
+            w_ref[step] = piece[...]
+        w_ref[3, : w3.shape[0]] = w3[...]
+        w_ref[3, w3.shape[0] :] = w4[...]
+
     join_rows(core_ref, own_ref, other_ref, x_ref)
     rows = x_ref[...].astype(f32)
     rms = rms_of(rows)
@@ -188,8 +195,9 @@
 
 def qkv_call(me, core, place, own, other, weights):
     places, half_tile, width = own.shape
-    half = weights.shape[1] * 128
+    half = weights[0].shape[0] * 128
     tile, count = 2 * half_tile, 2 * half_tile * places
+    all_shape = (BLOCKS,) + weights[0].shape
     row_spec = pl.BlockSpec((tile, width), lambda i, me, core, place: (i, 0))
     half_spec = pl.BlockSpec((tile, half), lambda i, me, core, place: (i, 0))
     part_spec = pl.BlockSpec(
@@ -202,25 +210,26 @@
         [
             part_spec,
             part_spec,
-            pl.BlockSpec(weights.shape, lambda i, me, core, place: (0, 0, 0, 0)),
-        ],
+        ]
+        + [pl.BlockSpec(w.shape, lambda i, me, core, place: (0, 0, 0)) for w in weights],
         [
             row_spec,
             row_spec,
             pl.BlockSpec((tile, 128), lambda i, me, core, place: (i, 0)),
             pl.BlockSpec((8, width), lambda i, me, core, place: (0, 0)),
+            pl.BlockSpec(all_shape, lambda i, me, core, place: (0, 0, 0, 0)),
             half_spec,
             half_spec,
             half_spec,
         ],
         [shaped((count, width), bf16)] * 2
-        + [shaped((count, 128), f32), shaped((8, width), f32)]
+        + [shaped((count, 128), f32), shaped((8, width), f32), shaped(all_shape, bf16)]
         + [shaped((count, half), bf16)] * 3,
         [],
         2 * count * width * half * 3,
         12 << 20,
         40,
-    )(me, core, place, own, other, weights)
+    )(me, core, place, own, other, *weights)
 
 
 def two_heads(rows):
@@ -340,13 +349,14 @@
     )(core, place, rows, one, two, gain, own, other)
 
 
-def ffn_kernel(given, prior, me_ref, normed_ref, d_out_ref, *refs):
+def ffn_kernel(given, prior, me_ref, core_ref, normed_ref, d_out_ref, *refs):
     pieces_of, refs = refs[:given], refs[given:]
     before = refs[:2] if prior else None
     refs = refs[2 if prior else 0 :]
     result_ref, d_normed_ref = refs[:2]
-    grad_refs = refs[2:6]
-    weights, inner_t, gate_t, up_t = refs[6:]
+    grad_refs, refs = refs[2:6], refs[6:]
+    give_ref = refs[0] if prior else None
+    weights, inner_t, gate_t, up_t = refs[1 if prior else 0 :]
     pieces, rows_all, wide = pieces_of[0].shape
     parts, kinds, depth = BLOCKS, 3, rows_all // 3
     units = pieces * depth
@@ -398,9 +408,18 @@
         for kind, (left, right) in enumerate(((gate_t, here), (up_t, here), (inner_t, there))):
             grad = dot_nn(left[...], right).astype(bf16)
             store_grad(grad_refs, step, grad.reshape(pieces, depth, wide), kind * depth)
-
-
-def ffn_call(me, normed, d_out, weights, *before):
+    if prior:
+        give_rows(core_ref, result_ref, give_ref)
+
+
+def give_rows(core_ref, all_ref, give_ref):
+    places, count = give_ref.shape[:2]
+    for place in range(places):
+        start = (2 * place + 1 - core_ref[0]) * count
+        give_ref[place] = all_ref[pl.ds(pl.multiple_of(start, count), count), :]
+
+
+def ffn_call(me, core, places, normed, d_out, weights, *before):
     count, width = normed.shape
     pieces, rows_all, wide = weights[0].shape
     units = pieces * rows_all // 3
@@ -408,15 +427,17 @@
     return call(
         functools.partial(ffn_kernel, len(weights), bool(before)),
         (),
-        1,
+        2,
         [whole] * (2 + len(weights) + len(before)),
-        [whole] * 6,
-        [shaped(normed.shape, bf16)] * 2 + grad_shapes(pieces, rows_all, wide),
+        [whole] * (7 if before else 6),
+        [shaped(normed.shape, bf16)] * 2
+        + grad_shapes(pieces, rows_all, wide)
+        + ([shaped((places, count // places // 2, width), bf16)] if before else []),
         [pltpu.VMEM((3, units, width), bf16)] + [pltpu.VMEM((units, count), bf16)] * 3,
         18 * count * width * units,
         20 << 20,
         56,
-    )(me, normed, d_out, *weights, *before)
+    )(me, core, normed, d_out, *weights, *before)
 
 
 def turn_kernel(
@@ -552,11 +573,13 @@
         dv_ref[...] = dv_sum[...].astype(bf16)
 
 
-def attend_back_call(flag, q, k, v, out, d_out, probs):
+def attend_back_call(first, pairs, flag, q, k, v, out, d_out, probs):
     count, half = q.shape
-    pairs, blocks = half // 128, count // SHORT
-    some = pl.BlockSpec((SHORT, 128), lambda j, i, flag: (i, j))
-    every = pl.BlockSpec((count, 128), lambda j, i, flag: (0, j))
+    blocks = count // SHORT
+    some = pl.BlockSpec((SHORT, 128), lambda j, i, flag: (i, j + first))
+    every = pl.BlockSpec((count, 128), lambda j, i, flag: (0, j + first))
+    some_out = pl.BlockSpec((SHORT, 128), lambda j, i, flag: (i, j))
+    every_out = pl.BlockSpec((count, 128), lambda j, i, flag: (0, j))
     return call(
         attend_back_kernel,
         (pairs, blocks),
@@ -567,74 +590,88 @@
             every,
             some,
             some,
-            pl.BlockSpec((1, 1, count, 2 * SHORT), lambda j, i, flag: (j, i, 0, 0)),
+            pl.BlockSpec((1, 1, count, 2 * SHORT), lambda j, i, flag: (j + first, i, 0, 0)),
         ],
-        [some, every, every],
-        [shaped(q.shape, bf16)] * 3,
+        [some_out, every_out, every_out],
+        [shaped((count, pairs * 128), bf16)] * 3,
         [pltpu.VMEM((128, count), bf16)] + [pltpu.VMEM((count, 128), f32)] * 2,
-        4 * 8 * count * count * half,
-        30 << 20,
+        4 * 8 * count * count * pairs * 128,
+        16 << 20,
         48,
     )(flag, q, k, v, out, d_out, probs)
 
 
 def square_kernel(
-    me_ref, dq_ref, dk_ref, dv_ref, att_ref, hidden_ref, d_branch_ref, w_ref, x_ref, rms_ref, line_ref, d_hidden_ref, *refs
+    me_ref,
+    core_ref,
+    dq_one,
+    dq_two,
+    dk_one,
+    dk_two,
+    dv_one,
+    dv_two,
+    att_ref,
+    hidden_ref,
+    d_branch_ref,
+    w_ref,
+    x_ref,
+    rms_ref,
+    line_ref,
+    d_hidden_ref,
+    give_ref,
+    *refs,
 ):
     grad_refs, turned = refs[:4], refs[4]
-    lefts = (dq_ref, dk_ref, dv_ref, att_ref)
-
-    @pl.when(pl.program_id(0) == 0)
-    def _():
-        for part, ref in enumerate(lefts):
-            turned[part] = ref[...].T
-
     pieces, wide = w_ref.shape[1], w_ref.shape[3]
-
-    def put(grad, first):
-        for step in range(BLOCKS):
-
-            @pl.when(pl.program_id(0) == step)
-            def _():
-                store_grad(grad_refs, step, grad, first)
-
-    total = None
-    for part, ref in enumerate(lefts):
-        rows = slice(part * 128, (part + 1) * 128)
-        right = d_branch_ref if part == 3 else hidden_ref
-        grad = dot_nn(turned[part], right[...])
-        put(grad.reshape(pieces, 128, wide).astype(bf16), part * 128)
-        if part < 3:
-            piece = dot_nn(ref[...], w_ref[0, :, rows, :].reshape(pieces * 128, wide))
+    lefts = (dq_one, dq_two, dk_one, dk_two, dv_one, dv_two)
+    start = 0
+    for ref in (*lefts, att_ref):
+        stop = start + ref.shape[1]
+        turned[start:stop, :] = ref[...].T
+        start = stop
+    half = att_ref.shape[1]
+    for step in range(BLOCKS):
+        columns = pl.ds(pl.multiple_of((me_ref[0] ^ step) * wide, wide), wide)
+        for part in range(4):
+            right = d_branch_ref if part == 3 else hidden_ref
+            grad = dot_nn(turned[part * half : (part + 1) * half, :], right[:, columns])
+            grad = grad.astype(bf16).reshape(pieces, 128, wide)
+            store_grad(grad_refs, step, grad, part * 128)
+        total = None
+        for index, ref in enumerate(lefts):
+            part, side = index // 2, index % 2 * pieces // 2
+            rows = slice(part * 128, (part + 1) * 128)
+            weight = w_ref[step, side : side + pieces // 2, rows, :].reshape(half // 2, wide)
+            piece = dot_nn(ref[...], weight)
             total = piece if total is None else total + piece
-    d_hidden_ref[...] = total.astype(bf16)
-    scaled = x_ref[...].astype(f32) * rms_ref[:, :1]
-    attn = jnp.sum(total * scaled, axis=0, keepdims=True)
-    lines = jnp.concatenate([attn, line_ref[...], jnp.zeros((14, wide), f32)], axis=0).astype(bf16)
-    put(jnp.broadcast_to(lines[None], (pieces, 16, wide)), 4 * 128)
-
-
-def square_call(me, dq, dk, dv, attended, hidden, d_branch, weights, x_rows, rms, line):
-    count, half = dq.shape
+        d_hidden_ref[:, columns] = total.astype(bf16)
+        scaled = x_ref[:, columns].astype(f32) * rms_ref[:, :1]
+        attn = jnp.sum(total * scaled, axis=0, keepdims=True)
+        lines = jnp.concatenate(
+            [attn, line_ref[:, columns], jnp.zeros((14, wide), f32)], axis=0
+        ).astype(bf16)
+        store_grad(grad_refs, step, jnp.broadcast_to(lines[None], (pieces, 16, wide)), 4 * 128)
+    give_rows(core_ref, d_hidden_ref, give_ref)
+
+
+def square_call(me, core, lefts, attended, hidden, d_branch, weights, x_rows, rms, line):
+    count, half = attended.shape
     width = hidden.shape[1]
-    parts, pieces, depth, wide = weights.shape
-    every = pl.BlockSpec((count, half), lambda d, me: (0, 0))
-    column = pl.BlockSpec((count, wide), lambda d, me: (0, me[0] ^ d))
+    pieces, depth, wide = weights.shape[1:]
+    whole = pl.BlockSpec(memory_space=pltpu.VMEM)
     return call(
         square_kernel,
-        (parts,),
-        1,
-        [every] * 4
-        + [column, column, pl.BlockSpec((1, pieces, depth, wide), lambda d, me: (d, 0, 0, 0))]
-        + [column, pl.BlockSpec(rms.shape, lambda d, me: (0, 0))]
-        + [pl.BlockSpec((1, wide), lambda d, me: (0, me[0] ^ d))],
-        [column] + [pl.BlockSpec((2, pieces // 2, depth, wide), lambda d, me: (0, 0, 0, 0))] * 4,
-        [shaped(hidden.shape, bf16)] + grad_shapes(pieces, depth, wide),
-        [pltpu.VMEM((4, half, count), bf16)],
+        (),
+        2,
+        [whole] * (len(lefts) + 7),
+        [whole] * 6,
+        [shaped(hidden.shape, bf16), shaped((pieces, count // pieces // 2, width), bf16)]
+        + grad_shapes(pieces, depth, wide),
+        [pltpu.VMEM((4 * half, count), bf16)],
         14 * count * width * half,
         24 << 20,
-        40,
-    )(me, dq, dk, dv, attended, hidden, d_branch, weights, x_rows, rms, line)
+        52,
+    )(me, core, *lefts, attended, hidden, d_branch, weights, x_rows, rms, line)
 
 
 def input_kernel(core_ref, x_ref, d_middle_ref, own_ref, other_ref, gain_ref, out_ref):
@@ -723,12 +760,26 @@
     def blocks_for(value):
         return [pick(value, turn(k), 0) for k in range(narrow)]
 
-    def across(blocks, *late):
+    far_place = narrow // 2
+
+    def across(blocks, near_late=(), far_late=(), sign=1):
         moved = [blocks[0]]
         for k in range(1, narrow):
-            block = stage(blocks[k], *late) if late and 2 * k == narrow else blocks[k]
-            moved.append(along(block, k))
+            late = far_late if k == far_place else near_late
+            moved.append(along(stage(blocks[k], *late) if late else blocks[k], sign * k))
         return moved
+
+    def across_near(blocks, sign=1):
+        return [along(blocks[k], sign * k) for k in range(1, narrow) if k != far_place]
+
+    def across_far(block, sign=1):
+        return along(block, sign * far_place)
+
+    def joined(own, near, far):
+        return [own] + near[: far_place - 1] + [far] + near[far_place - 1 :]
+
+    def near_of(moved):
+        return [moved[k] for k in range(1, narrow) if k != far_place]
 
     def in_order(moved):
         stacked = jnp.stack(moved)
@@ -764,7 +815,7 @@
         )
 
     def spread(value, *late):
-        return across([value] * narrow, *late)
+        return across([value] * narrow, (), late)
 
     near = chips == BLOCKS
 
@@ -804,7 +855,7 @@
         x_sum = x_keep[0].astype(f32) + got[0][0].astype(f32) + last[0].astype(f32)
         y_sum = y_keep[0].astype(f32) + got[1][0].astype(f32) + last[1].astype(f32)
         sent = [x_sum[k] for k in range(1, narrow // 2)] + [y_sum[k] for k in range(narrow // 2)]
-        return x_sum[0], [block.astype(bf16) for block in sent]
+        return x_sum[0], [None] + [block.astype(bf16) for block in sent]
 
     def sum_far(grads):
         x_keep, x_send, y_keep, y_send = grads
@@ -820,17 +871,11 @@
             tiled=True,
             axis_index_groups=same_core,
         ).reshape(value.shape[1:])
-        return got[0].astype(f32), [got[k] for k in range(1, narrow)]
-
-    def sum_places(sent, *late):
-        got = []
-        for k, block in enumerate(sent, 1):
-            got.append(along(stage(block, *late) if late and 2 * k == narrow else block, -k))
-        return got
+        return got[0].astype(f32), [None] + [got[k] for k in range(1, narrow)]
 
     def swap_ready(own, got):
         total = own
-        for piece in got:
+        for piece in got[1:]:
             total = total + piece.astype(f32)
         low, high = total[:, :own_width], total[:, own_width:]
         return jnp.where(by_core, low, high), jnp.where(by_core, high, low).astype(bf16)
@@ -891,9 +936,13 @@
     x_other = to_core(x_own)
     square_second = chips_second(*square_first) if near else ()
     one_z = spread(ffn_one, x_other)
-    square_full = chips_full(square_z, square_first, square_second)
-    x_rows, hidden, rms, gains, q, k, v = qkv_call(
-        me, core_index, place_index, x_own, x_other, square_full
+    x_rows, hidden, rms, gains, square_full, q, k, v = qkv_call(
+        me,
+        core_index,
+        place_index,
+        x_own,
+        x_other,
+        chips_pieces(square_z, square_first, square_second),
     )
 
     q, one_z, cot_blocks = stage((q, one_z, cot_blocks))
@@ -921,7 +970,7 @@
     two_z = jnp.stack(two_z)
     two_first = chips_first(two_z)
     part_result, part_d_normed, *one_grads = ffn_call(
-        me, normed, cot_rows, chips_pieces(one_z, one_first, one_second)
+        me, core_index, narrow, normed, cot_rows, chips_pieces(one_z, one_first, one_second)
     )
 
     part_result, part_d_normed, one_grads, two_first = stage(
@@ -933,8 +982,10 @@
         (part_result, part_d_normed, one_grads, two_second)
     )
     one_got = sum_first(one_grads) if near else ()
-    result, d_normed, *two_grads = ffn_call(
+    result, d_normed, *two_grads, result_give = ffn_call(
         me,
+        core_index,
+        narrow,
         normed,
         cot_rows,
         chips_pieces(two_z, two_first, two_second),
@@ -942,12 +993,10 @@
         part_d_normed,
     )
 
-    result, d_normed, two_grads, one_got = stage((result, d_normed, two_grads, one_got))
+    result_give, d_normed, one_got, two_grads = stage((result_give, d_normed, one_got, two_grads))
     by_rows = (narrow, 2, tile, width)
-    d_normed_other = to_core(d_normed)
+    d_normed_other, result_other = to_core(d_normed), to_core(result_give)
     one_last = sum_second(sum_ready(one_grads, one_got)) if near else ()
-    result = result.reshape(by_rows)
-    result_other = to_core(mine_of(result, 1)[1])
     d_middle, d_branch, d_att, ffn_gain_grad, out_rows = turn_call(
         me,
         core_index,
@@ -957,54 +1006,64 @@
         cot_rows,
         gains,
         square_full,
-        result,
+        result.reshape(by_rows),
         result_other,
     )
-    out_blocks = blocks_for(out_rows)
-
-    d_att, out_blocks, one_last, two_grads = stage((d_att, out_blocks, one_last, two_grads))
+    out_moved = across(blocks_for(out_rows))
+
+    d_att, one_last, two_grads = stage((d_att, one_last, two_grads))
     two_got = sum_first(two_grads) if near else ()
-    out_moved = across(out_blocks)
-    dq, dk, dv = attend_back_call(flag, q, k, v, attended, d_att, probs)
+    pairs = d_att.shape[1] // 256
+    lefts_one = attend_back_call(0, pairs, flag, q, k, v, attended, d_att, probs)
+
+    lefts_one, d_att, one_grads, one_got, one_last, two_grads, two_got = stage(
+        (lefts_one, d_att, one_grads, one_got, one_last, two_grads, two_got), near_of(out_moved)
+    )
+    two_last = sum_second(sum_ready(two_grads, two_got)) if near else ()
     one_own, one_sent = sum_done(one_grads, one_got, one_last) if near else sum_far(one_grads)
-
-    dq, one_sent, two_got, out_moved = stage((dq, one_sent, two_got, out_moved))
-    two_last = sum_second(sum_ready(two_grads, two_got)) if near else ()
-    one_places = sum_places(one_sent)
-    d_hidden, *square_grads = square_call(
-        me, dq, dk, dv, attended, hidden, d_branch, square_full, x_rows, rms, 0.5 * ffn_gain_grad
-    )
+    lefts_two = attend_back_call(pairs, pairs, flag, q, k, v, attended, d_att, probs)
+    one_near = across_near(one_sent, -1)
+
+    lefts_two, two_last, out_moved, one_near, one_far = stage(
+        (lefts_two, two_last, out_moved, one_near, one_sent[far_place])
+    )
+    one_places = joined(None, one_near, across_far(one_far, -1))
+    two_own, two_sent = sum_done(two_grads, two_got, two_last) if near else sum_far(two_grads)
+    two_sent[0] = two_own
+    two_places = across(two_sent, (), (), -1)
+    lefts = [left for both in zip(lefts_one, lefts_two) for left in both]
+    d_hidden, d_hidden_give, *square_grads = square_call(
+        me, core_index, lefts, attended, hidden, d_branch, square_full, x_rows, rms, 0.5 * ffn_gain_grad
+    )
+
+    d_hidden_give, square_grads, out_moved = stage(
+        (d_hidden_give, square_grads, out_moved), near_of(two_places), one_places[far_place]
+    )
+    square_got = sum_first(square_grads) if near else ()
+    d_hidden_other = to_core(d_hidden_give)
+    input_blocks = blocks_for(
+        input_call(
+            core_index, x_rows, d_middle, d_hidden.reshape(by_rows), d_hidden_other, gains
+        )
+    )
+    input_near = across_near(input_blocks)
     outputs = group_back(out_moved)
-
-    d_hidden, square_grads, two_last, one_places = stage(
-        (d_hidden, square_grads, two_last, one_places)
-    )
-    square_got = sum_first(square_grads) if near else ()
-    d_hidden = d_hidden.reshape(by_rows)
-    d_hidden_other = to_core(mine_of(d_hidden, 1)[1])
-    two_own, two_sent = sum_done(two_grads, two_got, two_last) if near else sum_far(two_grads)
-    two_places = sum_places(two_sent, d_hidden_other)
-    input_blocks = blocks_for(
-        input_call(core_index, x_rows, d_middle, d_hidden, d_hidden_other, gains)
-    )
     one_keep, one_swap = swap_ready(one_own, one_places)
 
-    input_blocks, square_got, two_places, one_swap = stage(
-        (input_blocks, square_got, two_places, one_swap)
-    )
+    square_got, one_swap, input_near, input_far, two_places = stage(
+        (square_got, one_swap, input_near, input_blocks[far_place], two_places)
+    )
+    input_moved = joined(input_blocks[0], input_near, across_far(input_far))
     square_last = sum_second(sum_ready(square_grads, square_got)) if near else ()
-    input_moved = across(input_blocks)
     one_theirs = to_core(one_swap)
     two_keep, two_swap = swap_ready(two_own, two_places)
-    two_theirs = to_core(two_swap)
-
-    square_last, input_moved, one_theirs, two_theirs = stage(
-        (square_last, input_moved, one_theirs, two_theirs)
-    )
+
+    square_last, input_moved, two_swap = stage((square_last, input_moved, two_swap))
     square_own, square_sent = (
         sum_done(square_grads, square_got, square_last) if near else sum_far(square_grads)
     )
-    square_places = sum_places(square_sent)
+    square_places = across(square_sent, (), (), -1)
+    two_theirs = to_core(two_swap)
     input_grad = group_back(input_moved).astype(f32)
     one_parts = finish(one_keep, one_theirs, 3, cut)
     two_parts = finish(two_keep, two_theirs, 3, depth - cut)

time: 427 us -> 409 us (0.958)
  Pallas kernels: 147 us -> 127 us
  other arithmetic: 31.7 us -> 20.9 us
  local copies, waits for them, and re-layouts: 40.6 us -> 47.3 us
  starting transfers between devices: 88.9 us -> 95.4 us
    ppermute x24, starting transfers between devices: 23.8 us -> 36.7 us  [to_chip(): return lax.ppermute(value, 'dp', [(i, i ^ 2 * flip) for i in range(dp)])]
    ppermute x30, waiting for transfers between devices: 73.8 us -> 62.6 us  [along(): lax.ppermute(value, 'narrow', [(i, (i + shift) % narrow) for i in range(n...]
    pallas_call x1, Pallas kernels: 24.9 us -> 15.4 us  [attend_call(): call(attend_kernel, (pairs, blocks), 1, [some, every, every], [some, pl.B...]
    pallas_call x1 -> x2, Pallas kernels: 30 us -> 21.3 us  [attend_back_call(): call(attend_back_kernel, (pairs, blocks), 1, [some, every, every, some, s...]
    ppermute x24, waiting for transfers between devices: 28.1 us -> 35.4 us  [to_chip(): return lax.ppermute(value, 'dp', [(i, i ^ 2 * flip) for i in range(dp)])]
    unnamed x156 -> x170, local copies, waits for them, and re-layouts: 27 us -> 33.7 us
    ppermute x30, starting transfers between devices: 61.5 us -> 55.1 us  [along(): lax.ppermute(value, 'narrow', [(i, (i + shift) % narrow) for i in range(n...]
    another operation x6 -> x4, other arithmetic: 7.92 us -> 2.82 us  [the longest x3 4.88 us: chips_full(): return jnp.stack([value, *firsts, jnp.concatenate(seconds)])]
  transfers between devices with their start and end apart: 69 -> 69, of which waited for: 24 -> 29; matrix products, arithmetic and copies ran while one was open for 9% -> 7% of each run, Pallas kernels for 35% -> 31%
where the time goes in v1:
time: 409 us; the launch traced here: 401 us
  Pallas kernels  127 us (31%)
  waiting for transfers between devices  109 us (27%)
  starting transfers between devices  95.4 us (23%)
  local copies, waits for them, and re-layouts  47.3 us (12%)
  other arithmetic  20.9 us (5%)
    ppermute x30, waiting for transfers between devices, along(): lax.ppermute(value, 'narrow', [(i, (i + shift) % narrow) for i in range(n...  62.6 us
    ppermute x30, starting transfers between devices, along(): lax.ppermute(value, 'narrow', [(i, (i + shift) % narrow) for i in range(n...  55.1 us
    pallas_call x2, Pallas kernels, ffn_call(): call(functools.partial(ffn_kernel, len(weights), bool(before)), (), 2, [w...  50.1 us
    ppermute x24, starting transfers between devices, to_chip(): return lax.ppermute(value, 'dp', [(i, i ^ 2 * flip) for i in range(dp)])  36.7 us
    ppermute x24, waiting for transfers between devices, to_chip(): return lax.ppermute(value, 'dp', [(i, i ^ 2 * flip) for i in range(dp)])  35.4 us
    unnamed x170, local copies, waits for them, and re-layouts  33.7 us
    pallas_call x2, Pallas kernels, attend_back_call(): call(attend_back_kernel, (pairs, blocks), 1, [some, every, every, some, s...  21.3 us
    pallas_call x1, Pallas kernels, square_call(): call(square_kernel, (), 2, [whole] * (len(lefts) + 7), [whole] * 6, [shap...  17.9 us
  transfers between devices with their start and end apart: 69, of which 29 were waited for; matrix products, arithmetic and copies ran while one was open for 7% of the time, Pallas kernels for 31%

profile of v1, /device:TPU:0, one launch (start us, length us, event | category | flops | bytes accessed | tf_op | source)
XLA Modules:
  0.0 401.5 jit_solution(14006598843586259383)
XLA Ops:
  8.3 3.0 collective-permute-start.1
  28.1 3.8 collective-permute-done.2
  38.2 4.1 %collective-permute-start.9 = (bf16[144,1024]{1,0:T(8,128)(2,1)S(1)}, bf16[144,1024]{1,0:T(8,128)(2,1)S(1)}, u32[]{:S(2)}, u32[]{:S(2)}) collective-permute-start(bf16[144,1024]{1,0:T(8,128)(2,1)S(1)} %get-tuple-element.223), channel_id=1, source_target_pairs={{0,1},{1,2},{2,3},{3,0},{4,5},{5,6},{6,7},{7,4},{8,9},{9,10},{10,1... | collective-permute-start | bytes 884744 | tf_op jit(solution)/shard_map/ppermute | solution.py:739
  44.7 6.8 %collective-permute-done.9 = bf16[144,1024]{1,0:T(8,128)(2,1)S(1)} collective-permute-done((bf16[144,1024]{1,0:T(8,128)(2,1)S(1)}, bf16[144,1024]{1,0:T(8,128)(2,1)S(1)}, u32[]{:S(2)}, u32[]{:S(2)}) %collective-permute-start.9) | collective-permute-done | bytes 294944 | tf_op jit(solution)/shard_map/ppermute | solution.py:739
  51.5 10.6 %collective-permute-done.10 = bf16[144,1024]{1,0:T(8,128)(2,1)S(1)} collective-permute-done((bf16[144,1024]{1,0:T(8,128)(2,1)S(1)}, bf16[144,1024]{1,0:T(8,128)(2,1)S(1)}, u32[]{:S(2)}, u32[]{:S(2)}) %collective-permute-start.10) | collective-permute-done | bytes 294944 | tf_op jit(solution)/shard_map/ppermute | solution.py:739
  65.9 6.8 %collective-permute-start.15 = (bf16[576,256]{1,0:T(8,128)(2,1)}, bf16[576,256]{1,0:T(8,128)(2,1)S(1)}, u32[]{:S(2)}, u32[]{:S(2)}) collective-permute-start(bf16[576,256]{1,0:T(8,128)(2,1)} %maximum_select_fusion.11), channel_id=1, source_target_pairs={{0,1},{1,2},{2,3},{3,0},{4,5},{5,6},{6,7},{7,4},{8,9},{9,10},{10,1... | collective-permute-start | bytes 884744 | tf_op jit(solution)/shard_map/ppermute | solution.py:739
  87.3 8.2 %shard_map.205 = (bf16[1152,1024]{1,0:T(8,128)(2,1)S(1)}, bf16[1152,1024]{1,0:T(8,128)(2,1)}, f32[1152,128]{1,0:T(8,128)S(1)}, f32[8,1024]{1,0:T(8,128)S(1)}, bf...) custom-call(s32[1]{0:T(128)} %bitcast.me_ref, ...), custom_call_target="tpu_custom_call" | custom-call | flops 3623878656 | bytes 12582912 | tf_op jit(solution)/shard_map/pallas_call | solution.py:206
  96.3 3.2 collective-permute-done.16
  107.9 15.4 %shard_map.206 = (bf16[1152,512]{1,0:T(8,128)(2,1)S(1)}, bf16[4,3,1152,768]{3,2,1,0:T(8,128)(2,1)}) custom-call(s32[1]{0:T(128)} %dynamic_slice.85.flag_ref, bf16[1152,512]{1,0:T(8,128)(2,1)S(1)} %get-tuple-element.240.q_ref, bf16[1152,512]{1,0:T(8,128)(2,1)S(1)} %get-tuple-element.241.k_ref, bf16[1152,512]{1,0:T(8,128)(2,1)S(1)} %get-tuple-element.242.v_ref), custom_call_target="tpu_custom_call" | custom-call | flops 10871635968 | bytes 29360128 | tf_op jit(solution)/shard_map/pallas_call | solution.py:277
  130.6 8.0 %collective-permute-start.24 = (bf16[2,576,256]{2,1,0:T(8,128)(2,1)S(1)}, bf16[2,576,256]{2,1,0:T(8,128)(2,1)S(1)}, u32[]{:S(2)}, u32[]{:S(2)}) collective-permute-start(bf16[2,576,256]{2,1,0:T(8,128)(2,1)S(1)} %slice.250), channel_id=1, source_target_pairs={{0,8},{4,12},{8,0},{12,4},{16,24},{20,28},{24,16},{28,20},{1,9},{5... | collective-permute-start | bytes 1769480 | tf_op jit(solution)/shard_map/ppermute | solution.py:736
  144.9 3.5 collective-permute-done.25
  152.1 3.9 collective-permute-done.28.other_ref
  167.2 24.2 %shard_map.209 = (bf16[1152,1024]{1,0:T(8,128)(2,1)}, bf16[1152,1024]{1,0:T(8,128)(2,1)}, bf16[2,2,576,256]{3,2,1,0:T(8,128)(2,1)}, bf16[2,2,576,256]{3,2,1,0:T(...) custom-call(s32[1]{0:T(128)} %bitcast.me_ref, s32[1]{0:T(128)} %bitcast.1.core_ref, ...), custom_call_target="tpu_custom_call" | custom-call | flops 16307453952 | bytes 20971520 | tf_op jit(solution)/shard_map/pallas_call | solution.py:427
  193.2 10.7 %collective-permute-done.32.refs_3_ = bf16[2,480,256]{2,1,0:T(8,128)(2,1)S(1)} collective-permute-done((bf16[2,480,256]{2,1,0:T(8,128)(2,1)S(1)}, bf16[2,480,256]{2,1,0:T(8,128)(2,1)S(1)}, u32[]{:S(2)}, u32[]{:S(2)}) %collective-permute-start.32) | collective-permute-done | bytes 491552 | tf_op jit(solution)/shard_map/ppermute | solution.py:736
  206.2 25.9 %shard_map.210 = (bf16[1152,1024]{1,0:T(8,128)(2,1)}, bf16[1152,1024]{1,0:T(8,128)(2,1)}, bf16[2,2,480,256]{3,2,1,0:T(8,128)(2,1)}, bf16[2,2,480,256]{3,2,1,0:T(...) custom-call(s32[1]{0:T(128)} %bitcast.me_ref, ...), custom_call_target="tpu_custom_call" | custom-call | flops 13589544960 | bytes 20971520 | tf_op jit(solution)/shard_map/pallas_call | solution.py:427
  240.3 8.1 %shard_map.211 = (f32[1152,1024]{1,0:T(8,128)}, bf16[1152,1024]{1,0:T(8,128)(2,1)S(1)}, bf16[1152,512]{1,0:T(8,128)(2,1)S(1)}, f32[1,1024]{1,0:T(1,128)S(1)}, bf16[4,144,1024]{2,1,0:T(8,128)(2,1)S(1)}) custom-call(s32[1]{0:T(128)} %bitcast.me_ref, s32[1]{0:T(128)} %bitcast.1.core_ref, f32[1152,1024]{1,0:T(8,128)} %copy-done.2, ...), custom_call_target="tpu_custom_call" | custom-call | flops 1207959552 | bytes 23068672 | tf_op jit(solution)/shard_map/pallas_call | solution.py:500
  253.1 3.8 collective-permute-start.43
  256.9 10.9 %shard_map.212 = (bf16[1152,256]{1,0:T(8,128)(2,1)S(1)}, bf16[1152,256]{1,0:T(8,128)(2,1)S(1)}, bf16[1152,256]{1,0:T(8,128)(2,1)S(1)}) custom-call(s32[1]{0:T(128)} %dynamic_slice.85.flag_ref, bf16[1152,512]{1,0:T(8,128)(2,1)S(1)} %copy-done.37, bf16[1152,512]{1,0:T(8,128)(2,1)S(1)} %copy-done.39, bf16[1152,512]{1,0:T(8,128)(2,1)S(1)} %copy-done.41, ...), custom_call_target="tpu_custom_call" | custom-call | flops 10871635968 | bytes 16777216 | tf_op jit(solution)/shard_map/pallas_call | solution.py:583
  269.3 4.2 %collective-permute-done.40 = bf16[2,2,480,256]{3,2,1,0:T(8,128)(2,1)S(1)} collective-permute-done((bf16[2,2,480,256]{3,2,1,0:T(8,128)(2,1)}, bf16[2,2,480,256]{3,2,1,0:T(8,128)(2,1)S(1)}, u32[]{:S(2)}, u32[]{:S(2)}) %collective-permute-start.40) | collective-permute-done | bytes 983072 | tf_op jit(solution)/shard_map/ppermute | solution.py:736
  281.1 10.4 %shard_map.213 = (bf16[1152,256]{1,0:T(8,128)(2,1)S(1)}, bf16[1152,256]{1,0:T(8,128)(2,1)S(1)}, bf16[1152,256]{1,0:T(8,128)(2,1)S(1)}) custom-call(s32[1]{0:T(128)} %dynamic_slice.85.flag_ref, bf16[1152,512]{1,0:T(8,128)(2,1)S(1)} %copy-done.37, bf16[1152,512]{1,0:T(8,128)(2,1)S(1)} %copy-done.39, bf16[1152,512]{1,0:T(8,128)(2,1)S(1)} %copy-done.41, ...), custom_call_target="tpu_custom_call" | custom-call | flops 10871635968 | bytes 16777216 | tf_op jit(solution)/shard_map/pallas_call | solution.py:583
  304.7 17.9 %shard_map.214 = (bf16[1152,1024]{1,0:T(8,128)(2,1)}, bf16[4,144,1024]{2,1,0:T(8,128)(2,1)}, bf16[2,2,528,256]{3,2,1,0:T(8,128)(2,1)}, bf16[2,2,528,256]{3,2,1,0...) custom-call(s32[1]{0:T(128)} %bitcast.me_ref, s32[1]{0:T(128)} %bitcast.1.core_ref, ...), custom_call_target="tpu_custom_call" | custom-call | flops 8455716864 | bytes 25165824 | tf_op jit(solution)/shard_map/pallas_call | solution.py:662
  339.9 11.3 %collective-permute-done.52 = bf16[2,2,528,256]{3,2,1,0:T(8,128)(2,1)S(1)} collective-permute-done((bf16[2,2,528,256]{3,2,1,0:T(8,128)(2,1)}, bf16[2,2,528,256]{3,2,1,0:T(8,128)(2,1)S(1)}, u32[]{:S(2)}, u32[]{:S(2)}) %collective-permute-start.52) | collective-permute-done | bytes 1081376 | tf_op jit(solution)/shard_map/ppermute | solution.py:736
  359.6 11.6 %collective-permute-done.60 = bf16[144,1024]{1,0:T(8,128)(2,1)S(1)} collective-permute-done((bf16[144,1024]{1,0:T(8,128)(2,1)S(1)}, bf16[144,1024]{1,0:T(8,128)(2,1)S(1)}, u32[]{:S(2)}, u32[]{:S(2)}) %collective-permute-start.60) | collective-permute-done | bytes 294944 | tf_op jit(solution)/shard_map/ppermute | solution.py:739
  381.9 14.2 %collective-permute-done.62 = bf16[528,256]{1,0:T(8,128)(2,1)S(1)} collective-permute-done((bf16[528,256]{1,0:T(8,128)(2,1)S(1)}, bf16[528,256]{1,0:T(8,128)(2,1)S(1)}, u32[]{:S(2)}, u32[]{:S(2)}) %collective-permute-start.62) | collective-permute-done | bytes 270368 | tf_op jit(solution)/shard_map/ppermute | solution.py:739
  (384 shorter events, 168.9 us)
Async XLA Ops:
  35.1 27.1 %collective-permute-start.7 = (bf16[4,528,256]{2,1,0:T(8,128)(2,1)S(1)}, bf16[4,528,256]{2,1,0:T(8,128)(2,1)S(1)}, u32[]{:S(2)}, u32[]{:S(2)}) collective-permute-start(bf16[4,528,256]{2,1,0:T(8,128)(2,1)S(1)} %pad_maximum_fusion.6.w0), channel_id=1, source_target_pairs={{0,8},{4,12},{8,0},{12,4},{16,24},{20,28},{24,16},{28,20},{1,9},{5... | collective-permute-start | bytes 3244040 | tf_op jit(solution)/shard_map/ppermute | solution.py:736
  36.7 25.5 %collective-permute-start.8 = (bf16[4,528,256]{2,1,0:T(8,128)(2,1)S(1)}, bf16[4,528,256]{2,1,0:T(8,128)(2,1)S(1)}, u32[]{:S(2)}, u32[]{:S(2)}) collective-permute-start(bf16[4,528,256]{2,1,0:T(8,128)(2,1)S(1)} %pad_maximum_fusion.6.w0), channel_id=1, source_target_pairs={{0,16},{4,20},{8,24},{12,28},{16,0},{20,4},{24,8},{28,12},{1,17},{... | collective-permute-start | bytes 3244040 | tf_op jit(solution)/shard_map/ppermute | solution.py:736
  65.9 30.5 %collective-permute-start.15 = (bf16[576,256]{1,0:T(8,128)(2,1)}, bf16[576,256]{1,0:T(8,128)(2,1)S(1)}, u32[]{:S(2)}, u32[]{:S(2)}) collective-permute-start(bf16[576,256]{1,0:T(8,128)(2,1)} %maximum_select_fusion.11), channel_id=1, source_target_pairs={{0,1},{1,2},{2,3},{3,0},{4,5},{5,6},{6,7},{7,4},{8,9},{9,10},{10,1... | collective-permute-start | bytes 884744 | tf_op jit(solution)/shard_map/ppermute | solution.py:739
  72.7 23.7 %collective-permute-start.17 = (bf16[576,256]{1,0:T(8,128)(2,1)}, bf16[576,256]{1,0:T(8,128)(2,1)S(1)}, u32[]{:S(2)}, u32[]{:S(2)}) collective-permute-start(bf16[576,256]{1,0:T(8,128)(2,1)} %maximum_select_fusion.11), channel_id=1, source_target_pairs={{0,3},{1,0},{2,1},{3,2},{4,7},{5,4},{6,5},{7,6},{8,11},{9,8},{10,9... | collective-permute-start | bytes 884744 | tf_op jit(solution)/shard_map/ppermute | solution.py:739
  75.0 24.5 %collective-permute-start.16 = (bf16[576,256]{1,0:T(8,128)(2,1)}, bf16[576,256]{1,0:T(8,128)(2,1)S(1)}, u32[]{:S(2)}, u32[]{:S(2)}) collective-permute-start(bf16[576,256]{1,0:T(8,128)(2,1)} %maximum_select_fusion.11), channel_id=1, source_target_pairs={{0,2},{1,3},{2,0},{3,1},{4,6},{5,7},{6,4},{7,5},{8,10},{9,11},{10,... | collective-permute-start | bytes 884744 | tf_op jit(solution)/shard_map/ppermute | solution.py:739
  99.7 28.0 %collective-permute-start.18 = (bf16[4,576,256]{2,1,0:T(8,128)(2,1)S(1)}, bf16[4,576,256]{2,1,0:T(8,128)(2,1)S(1)}, u32[]{:S(2)}, u32[]{:S(2)}) collective-permute-start(bf16[4,576,256]{2,1,0:T(8,128)(2,1)S(1)} %pad_maximum_fusion.1.refs_0_), channel_id=1, source_target_pairs={{0,8},{4,12},{8,0},{12,4},{16,24},{20,28},{24,16},{28,20},{1,9},{5... | collective-permute-start | bytes 3538952 | tf_op jit(solution)/shard_map/ppermute | solution.py:736
  101.3 27.6 %collective-permute-start.19 = (bf16[4,576,256]{2,1,0:T(8,128)(2,1)S(1)}, bf16[4,576,256]{2,1,0:T(8,128)(2,1)S(1)}, u32[]{:S(2)}, u32[]{:S(2)}) collective-permute-start(bf16[4,576,256]{2,1,0:T(8,128)(2,1)S(1)} %pad_maximum_fusion.1.refs_0_), channel_id=1, source_target_pairs={{0,16},{4,20},{8,24},{12,28},{16,0},{20,4},{24,8},{28,12},{1,17},{... | collective-permute-start | bytes 3538952 | tf_op jit(solution)/shard_map/ppermute | solution.py:736
  102.8 23.5 %collective-permute-start.20 = (bf16[144,1024]{1,0:T(8,128)(2,1)}, bf16[144,1024]{1,0:T(8,128)(2,1)S(1)}, u32[]{:S(2)}, u32[]{:S(2)}) collective-permute-start(bf16[144,1024]{1,0:T(8,128)(2,1)} %get-tuple-element.249), channel_id=1, source_target_pairs={{0,1},{1,2},{2,3},{3,0},{4,5},{5,6},{6,7},{7,4},{8,9},{9,10},{10,1... | collective-permute-start | bytes 884744 | tf_op jit(solution)/shard_map/ppermute | solution.py:739
  105.6 20.8 %collective-permute-start.21 = (bf16[144,1024]{1,0:T(8,128)(2,1)}, bf16[144,1024]{1,0:T(8,128)(2,1)S(1)}, u32[]{:S(2)}, u32[]{:S(2)}) collective-permute-start(bf16[144,1024]{1,0:T(8,128)(2,1)} %get-tuple-element.250), channel_id=1, source_target_pairs={{0,2},{1,3},{2,0},{3,1},{4,6},{5,7},{6,4},{7,5},{8,10},{9,11},{10,... | collective-permute-start | bytes 884744 | tf_op jit(solution)/shard_map/ppermute | solution.py:739
  164.6 26.8 %collective-permute-start.30 = (bf16[4,480,256]{2,1,0:T(8,128)(2,1)S(1)}, bf16[4,480,256]{2,1,0:T(8,128)(2,1)S(1)}, u32[]{:S(2)}, u32[]{:S(2)}) collective-permute-start(bf16[4,480,256]{2,1,0:T(8,128)(2,1)S(1)} %pad_maximum_fusion.7.refs_0_), channel_id=1, source_target_pairs={{0,8},{4,12},{8,0},{12,4},{16,24},{20,28},{24,16},{28,20},{1,9},{5... | collective-permute-start | bytes 2949128 | tf_op jit(solution)/shard_map/ppermute | solution.py:736
  166.2 25.2 %collective-permute-start.31 = (bf16[4,480,256]{2,1,0:T(8,128)(2,1)S(1)}, bf16[4,480,256]{2,1,0:T(8,128)(2,1)S(1)}, u32[]{:S(2)}, u32[]{:S(2)}) collective-permute-start(bf16[4,480,256]{2,1,0:T(8,128)(2,1)S(1)} %pad_maximum_fusion.7.refs_0_), channel_id=1, source_target_pairs={{0,16},{4,20},{8,24},{12,28},{16,0},{20,4},{24,8},{28,12},{1,17},{... | collective-permute-start | bytes 2949128 | tf_op jit(solution)/shard_map/ppermute | solution.py:736
  204.8 27.3 %collective-permute-start.34 = (bf16[2,2,576,256]{3,2,1,0:T(8,128)(2,1)}, bf16[2,2,576,256]{3,2,1,0:T(8,128)(2,1)S(1)}, u32[]{:S(2)}, u32[]{:S(2)}) collective-permute-start(bf16[2,2,576,256]{3,2,1,0:T(8,128)(2,1)} %get-tuple-element.300), channel_id=1, source_target_pairs={{0,8},{4,12},{8,0},{12,4},{16,24},{20,28},{24,16},{28,20},{1,9},{5... | collective-permute-start | bytes 3538952 | tf_op jit(solution)/shard_map/ppermute | solution.py:736
  205.2 26.9 %collective-permute-start.35 = (bf16[2,2,576,256]{3,2,1,0:T(8,128)(2,1)S(1)}, bf16[2,2,576,256]{3,2,1,0:T(8,128)(2,1)S(1)}, u32[]{:S(2)}, u32[]{:S(2)}) collective-permute-start(bf16[2,2,576,256]{3,2,1,0:T(8,128)(2,1)S(1)} %copy-done.78), channel_id=1, source_target_pairs={{0,16},{4,20},{8,24},{12,28},{16,0},{20,4},{24,8},{28,12},{1,17},{... | collective-permute-start | bytes 3538952 | tf_op jit(solution)/shard_map/ppermute | solution.py:736
  249.4 24.1 %collective-permute-start.40 = (bf16[2,2,480,256]{3,2,1,0:T(8,128)(2,1)}, bf16[2,2,480,256]{3,2,1,0:T(8,128)(2,1)S(1)}, u32[]{:S(2)}, u32[]{:S(2)}) collective-permute-start(bf16[2,2,480,256]{3,2,1,0:T(8,128)(2,1)} %get-tuple-element.326), channel_id=1, source_target_pairs={{0,8},{4,12},{8,0},{12,4},{16,24},{20,28},{24,16},{28,20},{1,9},{5... | collective-permute-start | bytes 2949128 | tf_op jit(solution)/shard_map/ppermute | solution.py:736
  251.1 23.7 %collective-permute-start.41 = (bf16[2,2,480,256]{3,2,1,0:T(8,128)(2,1)}, bf16[2,2,480,256]{3,2,1,0:T(8,128)(2,1)S(1)}, u32[]{:S(2)}, u32[]{:S(2)}) collective-permute-start(bf16[2,2,480,256]{3,2,1,0:T(8,128)(2,1)} %get-tuple-element.328), channel_id=1, source_target_pairs={{0,16},{4,20},{8,24},{12,28},{16,0},{20,4},{24,8},{28,12},{1,17},{... | collective-permute-start | bytes 2949128 | tf_op jit(solution)/shard_map/ppermute | solution.py:736
  256.9 34.6 %collective-permute-start.46 = (bf16[144,1024]{1,0:T(8,128)(2,1)}, bf16[144,1024]{1,0:T(8,128)(2,1)}, u32[]{:S(2)}, u32[]{:S(2)}) collective-permute-start(bf16[144,1024]{1,0:T(8,128)(2,1)} %get-tuple-element.415), channel_id=1, source_target_pairs={{0,2},{1,3},{2,0},{3,1},{4,6},{5,7},{6,4},{7,5},{8,10},{9,11},{10,... | collective-permute-start | bytes 884744 | tf_op jit(solution)/shard_map/ppermute | solution.py:739
  295.2 27.4 %collective-permute-start.49 = (bf16[480,256]{1,0:T(8,128)(2,1)S(1)}, bf16[480,256]{1,0:T(8,128)(2,1)S(1)}, u32[]{:S(2)}, u32[]{:S(2)}) collective-permute-start(bf16[480,256]{1,0:T(8,128)(2,1)S(1)} %fusion.17), channel_id=1, source_target_pairs={{0,3},{1,0},{2,1},{3,2},{4,7},{5,4},{6,5},{7,6},{8,11},{9,8},{10,9... | collective-permute-start | bytes 737288 | tf_op jit(solution)/shard_map/ppermute | solution.py:739
  299.6 23.0 %collective-permute-start.50 = (bf16[480,256]{1,0:T(8,128)(2,1)S(1)}, bf16[480,256]{1,0:T(8,128)(2,1)S(1)}, u32[]{:S(2)}, u32[]{:S(2)}) collective-permute-start(bf16[480,256]{1,0:T(8,128)(2,1)S(1)} %get-tuple-element.446), channel_id=1, source_target_pairs={{0,1},{1,2},{2,3},{3,0},{4,5},{5,6},{6,7},{7,4},{8,9},{9,10},{10,1... | collective-permute-start | bytes 737288 | tf_op jit(solution)/shard_map/ppermute | solution.py:739
  302.5 21.1 %collective-permute-start.51 = (bf16[576,256]{1,0:T(8,128)(2,1)S(1)}, bf16[576,256]{1,0:T(8,128)(2,1)S(1)}, u32[]{:S(2)}, u32[]{:S(2)}) collective-permute-start(bf16[576,256]{1,0:T(8,128)(2,1)S(1)} %get-tuple-element.365), channel_id=1, source_target_pairs={{0,2},{1,3},{2,0},{3,1},{4,6},{5,7},{6,4},{7,5},{8,10},{9,11},{10,... | collective-permute-start | bytes 884744 | tf_op jit(solution)/shard_map/ppermute | solution.py:739
  324.4 26.7 %collective-permute-start.52 = (bf16[2,2,528,256]{3,2,1,0:T(8,128)(2,1)}, bf16[2,2,528,256]{3,2,1,0:T(8,128)(2,1)S(1)}, u32[]{:S(2)}, u32[]{:S(2)}) collective-permute-start(bf16[2,2,528,256]{3,2,1,0:T(8,128)(2,1)} %get-tuple-element.367), channel_id=1, source_target_pairs={{0,8},{4,12},{8,0},{12,4},{16,24},{20,28},{24,16},{28,20},{1,9},{5... | collective-permute-start | bytes 3244040 | tf_op jit(solution)/shard_map/ppermute | solution.py:736
  326.7 25.9 %collective-permute-start.53 = (bf16[2,2,528,256]{3,2,1,0:T(8,128)(2,1)}, bf16[2,2,528,256]{3,2,1,0:T(8,128)(2,1)S(1)}, u32[]{:S(2)}, u32[]{:S(2)}) collective-permute-start(bf16[2,2,528,256]{3,2,1,0:T(8,128)(2,1)} %get-tuple-element.368), channel_id=1, source_target_pairs={{0,16},{4,20},{8,24},{12,28},{16,0},{20,4},{24,8},{28,12},{1,17},{... | collective-permute-start | bytes 3244040 | tf_op jit(solution)/shard_map/ppermute | solution.py:736
  339.8 35.4 %collective-permute-start.64 = (bf16[2,144,1024]{2,1,0:T(8,128)(2,1)S(1)}, bf16[2,144,1024]{2,1,0:T(8,128)(2,1)S(1)}, u32[]{:S(2)}, u32[]{:S(2)}) collective-permute-start(bf16[2,144,1024]{2,1,0:T(8,128)(2,1)S(1)} %maximum_select_fusion.5), channel_id=1, source_target_pairs={{0,4},{4,0},{8,12},{12,8},{16,20},{20,16},{24,28},{28,24},{1,5},{5... | collective-permute-start | bytes 1769480 | tf_op jit(solution)/shard_map/ppermute | solution.py:733
  373.9 22.1 %collective-permute-start.62 = (bf16[528,256]{1,0:T(8,128)(2,1)S(1)}, bf16[528,256]{1,0:T(8,128)(2,1)S(1)}, u32[]{:S(2)}, u32[]{:S(2)}) collective-permute-start(bf16[528,256]{1,0:T(8,128)(2,1)S(1)} %get-tuple-element.441), channel_id=1, source_target_pairs={{0,2},{1,3},{2,0},{3,1},{4,6},{5,7},{6,4},{7,5},{8,10},{9,11},{10,... | collective-permute-start | bytes 811016 | tf_op jit(solution)/shard_map/ppermute | solution.py:739
  374.0 22.1 %collective-permute-start.63 = (bf16[528,256]{1,0:T(8,128)(2,1)S(1)}, bf16[528,256]{1,0:T(8,128)(2,1)S(1)}, u32[]{:S(2)}, u32[]{:S(2)}) collective-permute-start(bf16[528,256]{1,0:T(8,128)(2,1)S(1)} %get-tuple-element.440), channel_id=1, source_target_pairs={{0,1},{1,2},{2,3},{3,0},{4,5},{5,6},{6,7},{7,4},{8,9},{9,10},{10,1... | collective-permute-start | bytes 811016 | tf_op jit(solution)/shard_map/ppermute | solution.py:739
  (130 other events, 1299.9 us)

commit v2 on v1

--- a/solution.py
+++ b/solution.py
@@ -284,7 +284,7 @@
         [pltpu.VMEM((128, count), bf16)],
         4 * 4 * count * count * half,
         28 << 20,
-        48,
+        40,
     )(flag, q, k, v)
 
 
@@ -436,7 +436,7 @@
         [pltpu.VMEM((3, units, width), bf16)] + [pltpu.VMEM((units, count), bf16)] * 3,
         18 * count * width * units,
         20 << 20,
-        56,
+        48,
     )(me, core, normed, d_out, *weights, *before)
 
 
@@ -465,9 +465,17 @@
     d_middle = cot_ref[...].astype(f32) + rms * (
         pulled - scaled * jnp.mean(pulled * scaled, axis=-1, keepdims=True)
     )
-    d_middle_ref[...] = d_middle
     d_branch_ref[...] = d_middle.astype(bf16)
     count = out_ref.shape[1]
+
+    @pl.when(core_ref[0] == 0)
+    def _():
+        d_middle_ref[0] = d_middle[:count]
+
+    @pl.when(core_ref[0] != 0)
+    def _():
+        d_middle_ref[0] = d_middle[count:]
+
     rows = pl.ds(pl.multiple_of(core_ref[0] * count, count), count)
     out_ref[0] = (
         middle_ref[rows, :] + (own_ref[0, 0].astype(f32) + other_ref[0].astype(f32))
@@ -504,9 +512,9 @@
         [spec, spec, spec, spec, gain_spec]
         + [pl.BlockSpec(block, lambda i, me, core: (0, 0, 3, 0))]
         + [pl.BlockSpec((1, 1, half_tile, width), lambda i, me, core: (i, core[0], 0, 0)), plain],
-        [spec, spec, pl.BlockSpec((tile, half), lambda i, me, core: (i, 0)), line, plain],
+        [plain, spec, pl.BlockSpec((tile, half), lambda i, me, core: (i, 0)), line, plain],
         [
-            shaped(middle.shape, f32),
+            shaped((places, half_tile, width), f32),
             shaped(middle.shape, bf16),
             shaped((count, half), bf16),
             shaped((1, width), f32),
@@ -597,7 +605,7 @@
         [pltpu.VMEM((128, count), bf16)] + [pltpu.VMEM((count, 128), f32)] * 2,
         4 * 8 * count * count * pairs * 128,
         16 << 20,
-        48,
+        40,
     )(flag, q, k, v, out, d_out, probs)
 
 
@@ -681,7 +689,7 @@
     d_hidden = own_ref[0, 0].astype(f32) + other_ref[0].astype(f32)
     pulled = d_hidden * gain_ref[:1, :]
     out_ref[0] = (
-        d_middle_ref[0, 0]
+        d_middle_ref[0]
         + rms * (pulled - scaled * jnp.mean(pulled * scaled, axis=-1, keepdims=True))
     ).astype(bf16)
 
@@ -694,14 +702,14 @@
         input_kernel,
         (slots,),
         1,
-        [mine, mine, mine, plain, pl.BlockSpec((8, width), lambda i, core: (0, 0))],
+        [mine, plain, mine, plain, pl.BlockSpec((8, width), lambda i, core: (0, 0))],
         plain,
         shaped((slots, tile, width), bf16),
         [],
         0,
         8 << 20,
         16,
-    )(core, rows.reshape(own.shape), d_middle.reshape(own.shape), own, other, gains)
+    )(core, rows.reshape(own.shape), d_middle, own, other, gains)
 
 
 def per_device(

time: 409 us -> 404 us (0.988)
  Pallas kernels: 127 us -> 145 us
  starting transfers between devices: 95.4 us -> 80.9 us
    ppermute x24, waiting for transfers between devices: 35.4 us -> 24.1 us  [to_chip(): return lax.ppermute(value, 'dp', [(i, i ^ 2 * flip) for i in range(dp)])]
    pallas_call x2, Pallas kernels: 21.3 us -> 32.4 us  [attend_back_call(): call(attend_back_kernel, (pairs, blocks), 1, [some, every, every, some, s...]
    ppermute x24, starting transfers between devices: 36.7 us -> 26 us  [to_chip(): return lax.ppermute(value, 'dp', [(i, i ^ 2 * flip) for i in range(dp)])]
    pallas_call x1, Pallas kernels: 15.4 us -> 24.9 us  [attend_call(): call(attend_kernel, (pairs, blocks), 1, [some, every, every], [some, pl.B...]
    ppermute x30, waiting for transfers between devices: 62.6 us -> 70.5 us  [along(): lax.ppermute(value, 'narrow', [(i, (i + shift) % narrow) for i in range(n...]
    unnamed x170 -> x160, local copies, waits for them, and re-layouts: 33.7 us -> 31.4 us
  transfers between devices with their start and end apart: 69 -> 69, of which waited for: 29 -> 28; matrix products, arithmetic and copies ran while one was open for 7% -> 6% of each run, Pallas kernels for 31% -> 36%
where the time goes in v2:
time: 404 us; the launch traced here: 397 us
  Pallas kernels  145 us (36%)
  waiting for transfers between devices  106 us (26%)
  starting transfers between devices  80.9 us (20%)
  local copies, waits for them, and re-layouts  44.9 us (11%)
  other arithmetic  18 us (4%)
    ppermute x30, waiting for transfers between devices, along(): lax.ppermute(value, 'narrow', [(i, (i + shift) % narrow) for i in range(n...  70.5 us
    ppermute x30, starting transfers between devices, along(): lax.ppermute(value, 'narrow', [(i, (i + shift) % narrow) for i in range(n...  51.4 us
    pallas_call x2, Pallas kernels, ffn_call(): call(functools.partial(ffn_kernel, len(weights), bool(before)), (), 2, [w...  48.5 us
    pallas_call x2, Pallas kernels, attend_back_call(): call(attend_back_kernel, (pairs, blocks), 1, [some, every, every, some, s...  32.4 us
    unnamed x160, local copies, waits for them, and re-layouts  31.4 us
    ppermute x24, starting transfers between devices, to_chip(): return lax.ppermute(value, 'dp', [(i, i ^ 2 * flip) for i in range(dp)])  26 us
    pallas_call x1, Pallas kernels, attend_call(): call(attend_kernel, (pairs, blocks), 1, [some, every, every], [some, pl.B...  24.9 us
    ppermute x24, waiting for transfers between devices, to_chip(): return lax.ppermute(value, 'dp', [(i, i ^ 2 * flip) for i in range(dp)])  24.1 us
  transfers between devices with their start and end apart: 69, of which 28 were waited for; matrix products, arithmetic and copies ran while one was open for 6% of the time, Pallas kernels for 36%

profile of v2, /device:TPU:0, one launch (start us, length us, event | category | flops | bytes accessed | tf_op | source)
XLA Modules:
  0.0 396.9 jit_solution(1383033212032490414)
XLA Ops:
  8.3 3.0 collective-permute-start.1
  28.1 3.8 collective-permute-done.2
  38.2 4.1 %collective-permute-start.9 = (bf16[144,1024]{1,0:T(8,128)(2,1)S(1)}, bf16[144,1024]{1,0:T(8,128)(2,1)S(1)}, u32[]{:S(2)}, u32[]{:S(2)}) collective-permute-start(bf16[144,1024]{1,0:T(8,128)(2,1)S(1)} %get-tuple-element.223), channel_id=1, source_target_pairs={{0,1},{1,2},{2,3},{3,0},{4,5},{5,6},{6,7},{7,4},{8,9},{9,10},{10,1... | collective-permute-start | bytes 884744 | tf_op jit(solution)/shard_map/ppermute | solution.py:747
  44.7 6.8 %collective-permute-done.9 = bf16[144,1024]{1,0:T(8,128)(2,1)S(1)} collective-permute-done((bf16[144,1024]{1,0:T(8,128)(2,1)S(1)}, bf16[144,1024]{1,0:T(8,128)(2,1)S(1)}, u32[]{:S(2)}, u32[]{:S(2)}) %collective-permute-start.9) | collective-permute-done | bytes 294944 | tf_op jit(solution)/shard_map/ppermute | solution.py:747
  51.5 10.6 %collective-permute-done.10 = bf16[144,1024]{1,0:T(8,128)(2,1)S(1)} collective-permute-done((bf16[144,1024]{1,0:T(8,128)(2,1)S(1)}, bf16[144,1024]{1,0:T(8,128)(2,1)S(1)}, u32[]{:S(2)}, u32[]{:S(2)}) %collective-permute-start.10) | collective-permute-done | bytes 294944 | tf_op jit(solution)/shard_map/ppermute | solution.py:747
  65.9 6.8 %collective-permute-start.15 = (bf16[576,256]{1,0:T(8,128)(2,1)}, bf16[576,256]{1,0:T(8,128)(2,1)S(1)}, u32[]{:S(2)}, u32[]{:S(2)}) collective-permute-start(bf16[576,256]{1,0:T(8,128)(2,1)} %maximum_select_fusion.11), channel_id=1, source_target_pairs={{0,1},{1,2},{2,3},{3,0},{4,5},{5,6},{6,7},{7,4},{8,9},{9,10},{10,1... | collective-permute-start | bytes 884744 | tf_op jit(solution)/shard_map/ppermute | solution.py:747
  87.3 8.2 %shard_map.205 = (bf16[1152,1024]{1,0:T(8,128)(2,1)S(1)}, bf16[1152,1024]{1,0:T(8,128)(2,1)}, f32[1152,128]{1,0:T(8,128)S(1)}, f32[8,1024]{1,0:T(8,128)S(1)}, bf...) custom-call(s32[1]{0:T(128)} %bitcast.me_ref, ...), custom_call_target="tpu_custom_call" | custom-call | flops 3623878656 | bytes 12582912 | tf_op jit(solution)/shard_map/pallas_call | solution.py:206
  96.3 3.3 collective-permute-done.16
  107.9 24.9 %shard_map.206 = (bf16[1152,512]{1,0:T(8,128)(2,1)S(1)}, bf16[4,3,1152,768]{3,2,1,0:T(8,128)(2,1)}) custom-call(s32[1]{0:T(128)} %dynamic_slice.85.flag_ref, bf16[1152,512]{1,0:T(8,128)(2,1)S(1)} %get-tuple-element.240.q_ref, bf16[1152,512]{1,0:T(8,128)(2,1)S(1)} %get-tuple-element.241.k_ref, bf16[1152,512]{1,0:T(8,128)(2,1)S(1)} %get-tuple-element.242.v_ref), custom_call_target="tpu_custom_call" | custom-call | flops 10871635968 | bytes 29360128 | tf_op jit(solution)/shard_map/pallas_call | solution.py:277
  144.5 3.4 collective-permute-done.25
  152.1 4.1 %collective-permute-done.28.other_ref = bf16[4,144,1024]{2,1,0:T(8,128)(2,1)S(1)} collective-permute-done((bf16[4,144,1024]{2,1,0:T(8,128)(2,1)S(1)}, bf16[4,144,1024]{2,1,0:T(8,128)(2,1)S(1)}, u32[]{:S(2)}, u32[]{:S(2)}) %collective-permute-start.28) | collective-permute-done | bytes 1179680 | tf_op jit(solution)/shard_map/ppermute | solution.py:741
  166.7 23.3 %shard_map.209 = (bf16[1152,1024]{1,0:T(8,128)(2,1)}, bf16[1152,1024]{1,0:T(8,128)(2,1)}, bf16[2,2,576,256]{3,2,1,0:T(8,128)(2,1)S(1)}, bf16[2,2,576,256]{3,2,1,...) custom-call(s32[1]{0:T(128)} %bitcast.me_ref, s32[1]{0:T(128)} %bitcast.1.core_ref, ...), custom_call_target="tpu_custom_call" | custom-call | flops 16307453952 | bytes 20971520 | tf_op jit(solution)/shard_map/pallas_call | solution.py:427
  192.3 10.2 %collective-permute-done.32.refs_3_ = bf16[2,480,256]{2,1,0:T(8,128)(2,1)S(1)} collective-permute-done((bf16[2,480,256]{2,1,0:T(8,128)(2,1)S(1)}, bf16[2,480,256]{2,1,0:T(8,128)(2,1)S(1)}, u32[]{:S(2)}, u32[]{:S(2)}) %collective-permute-start.32) | collective-permute-done | bytes 491552 | tf_op jit(solution)/shard_map/ppermute | solution.py:744
  205.3 25.2 %shard_map.210 = (bf16[1152,1024]{1,0:T(8,128)(2,1)}, bf16[1152,1024]{1,0:T(8,128)(2,1)}, bf16[2,2,480,256]{3,2,1,0:T(8,128)(2,1)S(1)}, bf16[2,2,480,256]{3,2,1,...) custom-call(s32[1]{0:T(128)} %bitcast.me_ref, ...), custom_call_target="tpu_custom_call" | custom-call | flops 13589544960 | bytes 20971520 | tf_op jit(solution)/shard_map/pallas_call | solution.py:427
  234.3 2.8 collective-permute-done.37.other_ref
  237.1 7.6 %shard_map.211 = (f32[4,144,1024]{2,1,0:T(8,128)S(1)}, bf16[1152,1024]{1,0:T(8,128)(2,1)S(1)}, bf16[1152,512]{1,0:T(8,128)(2,1)S(1)}, f32[1,1024]{1,0:T(1,128)S(1)}, bf16[4,144,1024]{2,1,0:T(8,128)(2,1)S(1)}) custom-call(s32[1]{0:T(128)} %bitcast.me_ref, s32[1]{0:T(128)} %bitcast.1.core_ref, f32[1152,1024]{1,0:T(8,128)} %copy-done.2, ...), custom_call_target="tpu_custom_call" | custom-call | flops 1207959552 | bytes 23068672 | tf_op jit(solution)/shard_map/pallas_call | solution.py:508
  251.5 3.8 collective-permute-start.43
  256.6 16.4 %shard_map.212 = (bf16[1152,256]{1,0:T(8,128)(2,1)S(1)}, bf16[1152,256]{1,0:T(8,128)(2,1)S(1)}, bf16[1152,256]{1,0:T(8,128)(2,1)S(1)}) custom-call(s32[1]{0:T(128)} %dynamic_slice.85.flag_ref, bf16[1152,512]{1,0:T(8,128)(2,1)S(1)} %copy-done.36, bf16[1152,512]{1,0:T(8,128)(2,1)S(1)} %copy-done.38, bf16[1152,512]{1,0:T(8,128)(2,1)S(1)} %copy-done.40, ...), custom_call_target="tpu_custom_call" | custom-call | flops 10871635968 | bytes 16777216 | tf_op jit(solution)/shard_map/pallas_call | solution.py:591
  278.8 16.0 %shard_map.213 = (bf16[1152,256]{1,0:T(8,128)(2,1)S(1)}, bf16[1152,256]{1,0:T(8,128)(2,1)S(1)}, bf16[1152,256]{1,0:T(8,128)(2,1)S(1)}) custom-call(s32[1]{0:T(128)} %dynamic_slice.85.flag_ref, bf16[1152,512]{1,0:T(8,128)(2,1)S(1)} %copy-done.36, bf16[1152,512]{1,0:T(8,128)(2,1)S(1)} %copy-done.38, bf16[1152,512]{1,0:T(8,128)(2,1)S(1)} %copy-done.40, ...), custom_call_target="tpu_custom_call" | custom-call | flops 10871635968 | bytes 16777216 | tf_op jit(solution)/shard_map/pallas_call | solution.py:591
  301.0 17.9 %shard_map.214 = (bf16[1152,1024]{1,0:T(8,128)(2,1)}, bf16[4,144,1024]{2,1,0:T(8,128)(2,1)}, bf16[2,2,528,256]{3,2,1,0:T(8,128)(2,1)}, bf16[2,2,528,256]{3,2,1,0...) custom-call(s32[1]{0:T(128)} %bitcast.me_ref, s32[1]{0:T(128)} %bitcast.1.core_ref, ...), custom_call_target="tpu_custom_call" | custom-call | flops 8455716864 | bytes 25165824 | tf_op jit(solution)/shard_map/pallas_call | solution.py:670
  333.2 9.6 %collective-permute-done.57 = bf16[480,256]{1,0:T(8,128)(2,1)S(1)} collective-permute-done((bf16[480,256]{1,0:T(8,128)(2,1)}, bf16[480,256]{1,0:T(8,128)(2,1)S(1)}, u32[]{:S(2)}, u32[]{:S(2)}) %collective-permute-start.57) | collective-permute-done | bytes 245792 | tf_op jit(solution)/shard_map/ppermute | solution.py:747
  342.9 4.9 %collective-permute-done.52 = bf16[2,2,528,256]{3,2,1,0:T(8,128)(2,1)S(1)} collective-permute-done((bf16[2,2,528,256]{3,2,1,0:T(8,128)(2,1)}, bf16[2,2,528,256]{3,2,1,0:T(8,128)(2,1)S(1)}, u32[]{:S(2)}, u32[]{:S(2)}) %collective-permute-start.52) | collective-permute-done | bytes 1081376 | tf_op jit(solution)/shard_map/ppermute | solution.py:744
  354.7 12.1 %collective-permute-done.60 = bf16[144,1024]{1,0:T(8,128)(2,1)S(1)} collective-permute-done((bf16[144,1024]{1,0:T(8,128)(2,1)S(1)}, bf16[144,1024]{1,0:T(8,128)(2,1)S(1)}, u32[]{:S(2)}, u32[]{:S(2)}) %collective-permute-start.60) | collective-permute-done | bytes 294944 | tf_op jit(solution)/shard_map/ppermute | solution.py:747
  377.3 14.2 %collective-permute-done.62 = bf16[528,256]{1,0:T(8,128)(2,1)S(1)} collective-permute-done((bf16[528,256]{1,0:T(8,128)(2,1)S(1)}, bf16[528,256]{1,0:T(8,128)(2,1)S(1)}, u32[]{:S(2)}, u32[]{:S(2)}) %collective-permute-start.62) | collective-permute-done | bytes 270368 | tf_op jit(solution)/shard_map/ppermute | solution.py:747
  (374 shorter events, 151.8 us)
Async XLA Ops:
  35.1 27.1 %collective-permute-start.7 = (bf16[4,528,256]{2,1,0:T(8,128)(2,1)S(1)}, bf16[4,528,256]{2,1,0:T(8,128)(2,1)S(1)}, u32[]{:S(2)}, u32[]{:S(2)}) collective-permute-start(bf16[4,528,256]{2,1,0:T(8,128)(2,1)S(1)} %pad_maximum_fusion.6.w0), channel_id=1, source_target_pairs={{0,8},{4,12},{8,0},{12,4},{16,24},{20,28},{24,16},{28,20},{1,9},{5... | collective-permute-start | bytes 3244040 | tf_op jit(solution)/shard_map/ppermute | solution.py:744
  36.7 25.5 %collective-permute-start.8 = (bf16[4,528,256]{2,1,0:T(8,128)(2,1)S(1)}, bf16[4,528,256]{2,1,0:T(8,128)(2,1)S(1)}, u32[]{:S(2)}, u32[]{:S(2)}) collective-permute-start(bf16[4,528,256]{2,1,0:T(8,128)(2,1)S(1)} %pad_maximum_fusion.6.w0), channel_id=1, source_target_pairs={{0,16},{4,20},{8,24},{12,28},{16,0},{20,4},{24,8},{28,12},{1,17},{... | collective-permute-start | bytes 3244040 | tf_op jit(solution)/shard_map/ppermute | solution.py:744
  65.9 30.4 %collective-permute-start.15 = (bf16[576,256]{1,0:T(8,128)(2,1)}, bf16[576,256]{1,0:T(8,128)(2,1)S(1)}, u32[]{:S(2)}, u32[]{:S(2)}) collective-permute-start(bf16[576,256]{1,0:T(8,128)(2,1)} %maximum_select_fusion.11), channel_id=1, source_target_pairs={{0,1},{1,2},{2,3},{3,0},{4,5},{5,6},{6,7},{7,4},{8,9},{9,10},{10,1... | collective-permute-start | bytes 884744 | tf_op jit(solution)/shard_map/ppermute | solution.py:747
  72.7 23.6 %collective-permute-start.17 = (bf16[576,256]{1,0:T(8,128)(2,1)}, bf16[576,256]{1,0:T(8,128)(2,1)S(1)}, u32[]{:S(2)}, u32[]{:S(2)}) collective-permute-start(bf16[576,256]{1,0:T(8,128)(2,1)} %maximum_select_fusion.11), channel_id=1, source_target_pairs={{0,3},{1,0},{2,1},{3,2},{4,7},{5,4},{6,5},{7,6},{8,11},{9,8},{10,9... | collective-permute-start | bytes 884744 | tf_op jit(solution)/shard_map/ppermute | solution.py:747
  75.0 24.6 %collective-permute-start.16 = (bf16[576,256]{1,0:T(8,128)(2,1)}, bf16[576,256]{1,0:T(8,128)(2,1)S(1)}, u32[]{:S(2)}, u32[]{:S(2)}) collective-permute-start(bf16[576,256]{1,0:T(8,128)(2,1)} %maximum_select_fusion.11), channel_id=1, source_target_pairs={{0,2},{1,3},{2,0},{3,1},{4,6},{5,7},{6,4},{7,5},{8,10},{9,11},{10,... | collective-permute-start | bytes 884744 | tf_op jit(solution)/shard_map/ppermute | solution.py:747
  99.7 36.2 %collective-permute-start.18 = (bf16[4,576,256]{2,1,0:T(8,128)(2,1)S(1)}, bf16[4,576,256]{2,1,0:T(8,128)(2,1)S(1)}, u32[]{:S(2)}, u32[]{:S(2)}) collective-permute-start(bf16[4,576,256]{2,1,0:T(8,128)(2,1)S(1)} %pad_maximum_fusion.1.refs_0_), channel_id=1, source_target_pairs={{0,8},{4,12},{8,0},{12,4},{16,24},{20,28},{24,16},{28,20},{1,9},{5... | collective-permute-start | bytes 3538952 | tf_op jit(solution)/shard_map/ppermute | solution.py:744
  101.3 34.6 %collective-permute-start.19 = (bf16[4,576,256]{2,1,0:T(8,128)(2,1)S(1)}, bf16[4,576,256]{2,1,0:T(8,128)(2,1)S(1)}, u32[]{:S(2)}, u32[]{:S(2)}) collective-permute-start(bf16[4,576,256]{2,1,0:T(8,128)(2,1)S(1)} %pad_maximum_fusion.1.refs_0_), channel_id=1, source_target_pairs={{0,16},{4,20},{8,24},{12,28},{16,0},{20,4},{24,8},{28,12},{1,17},{... | collective-permute-start | bytes 3538952 | tf_op jit(solution)/shard_map/ppermute | solution.py:744
  102.8 33.1 %collective-permute-start.20 = (bf16[144,1024]{1,0:T(8,128)(2,1)S(1)}, bf16[144,1024]{1,0:T(8,128)(2,1)S(1)}, u32[]{:S(2)}, u32[]{:S(2)}) collective-permute-start(bf16[144,1024]{1,0:T(8,128)(2,1)S(1)} %copy-done.69), channel_id=1, source_target_pairs={{0,1},{1,2},{2,3},{3,0},{4,5},{5,6},{6,7},{7,4},{8,9},{9,10},{10,1... | collective-permute-start | bytes 884744 | tf_op jit(solution)/shard_map/ppermute | solution.py:747
  105.5 30.4 %collective-permute-start.21 = (bf16[144,1024]{1,0:T(8,128)(2,1)S(1)}, bf16[144,1024]{1,0:T(8,128)(2,1)S(1)}, u32[]{:S(2)}, u32[]{:S(2)}) collective-permute-start(bf16[144,1024]{1,0:T(8,128)(2,1)S(1)} %copy-done.68), channel_id=1, source_target_pairs={{0,2},{1,3},{2,0},{3,1},{4,6},{5,7},{6,4},{7,5},{8,10},{9,11},{10,... | collective-permute-start | bytes 884744 | tf_op jit(solution)/shard_map/ppermute | solution.py:747
  107.2 28.7 %collective-permute-start.22 = (bf16[144,1024]{1,0:T(8,128)(2,1)S(1)}, bf16[144,1024]{1,0:T(8,128)(2,1)S(1)}, u32[]{:S(2)}, u32[]{:S(2)}) collective-permute-start(bf16[144,1024]{1,0:T(8,128)(2,1)S(1)} %copy-done.67), channel_id=1, source_target_pairs={{0,3},{1,0},{2,1},{3,2},{4,7},{5,4},{6,5},{7,6},{8,11},{9,8},{10,9... | collective-permute-start | bytes 884744 | tf_op jit(solution)/shard_map/ppermute | solution.py:747
  164.6 25.4 %collective-permute-start.30 = (bf16[4,480,256]{2,1,0:T(8,128)(2,1)S(1)}, bf16[4,480,256]{2,1,0:T(8,128)(2,1)S(1)}, u32[]{:S(2)}, u32[]{:S(2)}) collective-permute-start(bf16[4,480,256]{2,1,0:T(8,128)(2,1)S(1)} %pad_maximum_fusion.7.refs_0_), channel_id=1, source_target_pairs={{0,8},{4,12},{8,0},{12,4},{16,24},{20,28},{24,16},{28,20},{1,9},{5... | collective-permute-start | bytes 2949128 | tf_op jit(solution)/shard_map/ppermute | solution.py:744
  165.6 24.4 %collective-permute-start.31 = (bf16[4,480,256]{2,1,0:T(8,128)(2,1)S(1)}, bf16[4,480,256]{2,1,0:T(8,128)(2,1)S(1)}, u32[]{:S(2)}, u32[]{:S(2)}) collective-permute-start(bf16[4,480,256]{2,1,0:T(8,128)(2,1)S(1)} %pad_maximum_fusion.7.refs_0_), channel_id=1, source_target_pairs={{0,16},{4,20},{8,24},{12,28},{16,0},{20,4},{24,8},{28,12},{1,17},{... | collective-permute-start | bytes 2949128 | tf_op jit(solution)/shard_map/ppermute | solution.py:744
  203.2 27.3 %collective-permute-start.34 = (bf16[2,2,576,256]{3,2,1,0:T(8,128)(2,1)S(1)}, bf16[2,2,576,256]{3,2,1,0:T(8,128)(2,1)S(1)}, u32[]{:S(2)}, u32[]{:S(2)}) collective-permute-start(bf16[2,2,576,256]{3,2,1,0:T(8,128)(2,1)S(1)} %get-tuple-element.300), channel_id=1, source_target_pairs={{0,8},{4,12},{8,0},{12,4},{16,24},{20,28},{24,16},{28,20},{1,9},{5... | collective-permute-start | bytes 3538952 | tf_op jit(solution)/shard_map/ppermute | solution.py:744
  204.4 26.2 %collective-permute-start.35 = (bf16[2,2,576,256]{3,2,1,0:T(8,128)(2,1)S(1)}, bf16[2,2,576,256]{3,2,1,0:T(8,128)(2,1)S(1)}, u32[]{:S(2)}, u32[]{:S(2)}) collective-permute-start(bf16[2,2,576,256]{3,2,1,0:T(8,128)(2,1)S(1)} %get-tuple-element.301), channel_id=1, source_target_pairs={{0,16},{4,20},{8,24},{12,28},{16,0},{20,4},{24,8},{28,12},{1,17},{... | collective-permute-start | bytes 3538952 | tf_op jit(solution)/shard_map/ppermute | solution.py:744
  248.7 24.4 %collective-permute-start.40 = (bf16[2,2,480,256]{3,2,1,0:T(8,128)(2,1)S(1)}, bf16[2,2,480,256]{3,2,1,0:T(8,128)(2,1)S(1)}, u32[]{:S(2)}, u32[]{:S(2)}) collective-permute-start(bf16[2,2,480,256]{3,2,1,0:T(8,128)(2,1)S(1)} %copy-done.30), channel_id=1, source_target_pairs={{0,8},{4,12},{8,0},{12,4},{16,24},{20,28},{24,16},{28,20},{1,9},{5... | collective-permute-start | bytes 2949128 | tf_op jit(solution)/shard_map/ppermute | solution.py:744
  249.5 23.6 %collective-permute-start.41 = (bf16[2,2,480,256]{3,2,1,0:T(8,128)(2,1)S(1)}, bf16[2,2,480,256]{3,2,1,0:T(8,128)(2,1)S(1)}, u32[]{:S(2)}, u32[]{:S(2)}) collective-permute-start(bf16[2,2,480,256]{3,2,1,0:T(8,128)(2,1)S(1)} %get-tuple-element.328), channel_id=1, source_target_pairs={{0,16},{4,20},{8,24},{12,28},{16,0},{20,4},{24,8},{28,12},{1,17},{... | collective-permute-start | bytes 2949128 | tf_op jit(solution)/shard_map/ppermute | solution.py:744
  255.3 39.5 %collective-permute-start.46 = (bf16[144,1024]{1,0:T(8,128)(2,1)S(1)}, bf16[144,1024]{1,0:T(8,128)(2,1)S(1)}, u32[]{:S(2)}, u32[]{:S(2)}) collective-permute-start(bf16[144,1024]{1,0:T(8,128)(2,1)S(1)} %get-tuple-element.415), channel_id=1, source_target_pairs={{0,2},{1,3},{2,0},{3,1},{4,6},{5,7},{6,4},{7,5},{8,10},{9,11},{10,... | collective-permute-start | bytes 884744 | tf_op jit(solution)/shard_map/ppermute | solution.py:747
  296.1 22.8 %collective-permute-start.49 = (bf16[480,256]{1,0:T(8,128)(2,1)S(1)}, bf16[480,256]{1,0:T(8,128)(2,1)S(1)}, u32[]{:S(2)}, u32[]{:S(2)}) collective-permute-start(bf16[480,256]{1,0:T(8,128)(2,1)S(1)} %fusion.17), channel_id=1, source_target_pairs={{0,3},{1,0},{2,1},{3,2},{4,7},{5,4},{6,5},{7,6},{8,11},{9,8},{10,9... | collective-permute-start | bytes 737288 | tf_op jit(solution)/shard_map/ppermute | solution.py:747
  321.3 21.6 %collective-permute-start.57 = (bf16[480,256]{1,0:T(8,128)(2,1)}, bf16[480,256]{1,0:T(8,128)(2,1)S(1)}, u32[]{:S(2)}, u32[]{:S(2)}) collective-permute-start(bf16[480,256]{1,0:T(8,128)(2,1)} %get-tuple-element.445), channel_id=1, source_target_pairs={{0,2},{1,3},{2,0},{3,1},{4,6},{5,7},{6,4},{7,5},{8,10},{9,11},{10,... | collective-permute-start | bytes 737288 | tf_op jit(solution)/shard_map/ppermute | solution.py:747
  321.6 26.2 %collective-permute-start.52 = (bf16[2,2,528,256]{3,2,1,0:T(8,128)(2,1)}, bf16[2,2,528,256]{3,2,1,0:T(8,128)(2,1)S(1)}, u32[]{:S(2)}, u32[]{:S(2)}) collective-permute-start(bf16[2,2,528,256]{3,2,1,0:T(8,128)(2,1)} %get-tuple-element.367), channel_id=1, source_target_pairs={{0,8},{4,12},{8,0},{12,4},{16,24},{20,28},{24,16},{28,20},{1,9},{5... | collective-permute-start | bytes 3244040 | tf_op jit(solution)/shard_map/ppermute | solution.py:744
  322.4 25.9 %collective-permute-start.53 = (bf16[2,2,528,256]{3,2,1,0:T(8,128)(2,1)}, bf16[2,2,528,256]{3,2,1,0:T(8,128)(2,1)S(1)}, u32[]{:S(2)}, u32[]{:S(2)}) collective-permute-start(bf16[2,2,528,256]{3,2,1,0:T(8,128)(2,1)} %get-tuple-element.368), channel_id=1, source_target_pairs={{0,16},{4,20},{8,24},{12,28},{16,0},{20,4},{24,8},{28,12},{1,17},{... | collective-permute-start | bytes 3244040 | tf_op jit(solution)/shard_map/ppermute | solution.py:744
  342.8 27.8 %collective-permute-start.64 = (bf16[2,144,1024]{2,1,0:T(8,128)(2,1)S(1)}, bf16[2,144,1024]{2,1,0:T(8,128)(2,1)S(1)}, u32[]{:S(2)}, u32[]{:S(2)}) collective-permute-start(bf16[2,144,1024]{2,1,0:T(8,128)(2,1)S(1)} %maximum_select_fusion.5), channel_id=1, source_target_pairs={{0,4},{4,0},{8,12},{12,8},{16,20},{20,16},{24,28},{28,24},{1,5},{5... | collective-permute-start | bytes 1769480 | tf_op jit(solution)/shard_map/ppermute | solution.py:741
  369.3 22.1 %collective-permute-start.62 = (bf16[528,256]{1,0:T(8,128)(2,1)S(1)}, bf16[528,256]{1,0:T(8,128)(2,1)S(1)}, u32[]{:S(2)}, u32[]{:S(2)}) collective-permute-start(bf16[528,256]{1,0:T(8,128)(2,1)S(1)} %get-tuple-element.441), channel_id=1, source_target_pairs={{0,2},{1,3},{2,0},{3,1},{4,6},{5,7},{6,4},{7,5},{8,10},{9,11},{10,... | collective-permute-start | bytes 811016 | tf_op jit(solution)/shard_map/ppermute | solution.py:747
  369.4 22.1 %collective-permute-start.63 = (bf16[528,256]{1,0:T(8,128)(2,1)S(1)}, bf16[528,256]{1,0:T(8,128)(2,1)S(1)}, u32[]{:S(2)}, u32[]{:S(2)}) collective-permute-start(bf16[528,256]{1,0:T(8,128)(2,1)S(1)} %get-tuple-element.440), channel_id=1, source_target_pairs={{0,1},{1,2},{2,3},{3,0},{4,5},{5,6},{6,7},{7,4},{8,9},{9,10},{10,1... | collective-permute-start | bytes 811016 | tf_op jit(solution)/shard_map/ppermute | solution.py:747
  (125 other events, 1323.7 us)

commit v3 on v2

--- a/solution.py
+++ b/solution.py
@@ -284,7 +284,7 @@
         [pltpu.VMEM((128, count), bf16)],
         4 * 4 * count * count * half,
         28 << 20,
-        40,
+        32,
     )(flag, q, k, v)
 
 
@@ -605,7 +605,7 @@
         [pltpu.VMEM((128, count), bf16)] + [pltpu.VMEM((count, 128), f32)] * 2,
         4 * 8 * count * count * pairs * 128,
         16 << 20,
-        40,
+        32,
     )(flag, q, k, v, out, d_out, probs)
 
 

time: 404 us -> 404 us (level)
    unnamed x160 -> x156, local copies, waits for them, and re-layouts: 31.4 us -> 32.4 us
  transfers between devices with their start and end apart: 69 -> 69, of which waited for: 28 -> 27; matrix products, arithmetic and copies ran while one was open for 6% -> 6% of each run, Pallas kernels for 36% -> 36%
where the time goes in v3:
time: 404 us; the launch traced here: 396 us
  Pallas kernels  145 us (36%)
  waiting for transfers between devices  105 us (26%)
  starting transfers between devices  81.1 us (20%)
  local copies, waits for them, and re-layouts  45.9 us (11%)
  other arithmetic  17.1 us (4%)
    ppermute x30, waiting for transfers between devices, along(): lax.ppermute(value, 'narrow', [(i, (i + shift) % narrow) for i in range(n...  68.8 us
    ppermute x30, starting transfers between devices, along(): lax.ppermute(value, 'narrow', [(i, (i + shift) % narrow) for i in range(n...  50.4 us
    pallas_call x2, Pallas kernels, ffn_call(): call(functools.partial(ffn_kernel, len(weights), bool(before)), (), 2, [w...  48.4 us
    pallas_call x2, Pallas kernels, attend_back_call(): call(attend_back_kernel, (pairs, blocks), 1, [some, every, every, some, s...  32.4 us
    unnamed x156, local copies, waits for them, and re-layouts  32.4 us
    ppermute x24, starting transfers between devices, to_chip(): return lax.ppermute(value, 'dp', [(i, i ^ 2 * flip) for i in range(dp)])  27.1 us
    pallas_call x1, Pallas kernels, attend_call(): call(attend_kernel, (pairs, blocks), 1, [some, every, every], [some, pl.B...  24.9 us
    ppermute x24, waiting for transfers between devices, to_chip(): return lax.ppermute(value, 'dp', [(i, i ^ 2 * flip) for i in range(dp)])  24.6 us
  transfers between devices with their start and end apart: 69, of which 27 were waited for; matrix products, arithmetic and copies ran while one was open for 6% of the time, Pallas kernels for 36%

profile of v3, /device:TPU:0, one launch (start us, length us, event | category | flops | bytes accessed | tf_op | source)
XLA Modules:
  0.0 396.3 jit_solution(12857165244000788809)
XLA Ops:
  28.1 3.8 collective-permute-done.2
  38.2 4.1 %collective-permute-start.9 = (bf16[144,1024]{1,0:T(8,128)(2,1)S(1)}, bf16[144,1024]{1,0:T(8,128)(2,1)S(1)}, u32[]{:S(2)}, u32[]{:S(2)}) collective-permute-start(bf16[144,1024]{1,0:T(8,128)(2,1)S(1)} %get-tuple-element.223), channel_id=1, source_target_pairs={{0,1},{1,2},{2,3},{3,0},{4,5},{5,6},{6,7},{7,4},{8,9},{9,10},{10,1... | collective-permute-start | bytes 884744 | tf_op jit(solution)/shard_map/ppermute | solution.py:747
  44.7 6.8 %collective-permute-done.9 = bf16[144,1024]{1,0:T(8,128)(2,1)S(1)} collective-permute-done((bf16[144,1024]{1,0:T(8,128)(2,1)S(1)}, bf16[144,1024]{1,0:T(8,128)(2,1)S(1)}, u32[]{:S(2)}, u32[]{:S(2)}) %collective-permute-start.9) | collective-permute-done | bytes 294944 | tf_op jit(solution)/shard_map/ppermute | solution.py:747
  51.5 10.6 %collective-permute-done.10 = bf16[144,1024]{1,0:T(8,128)(2,1)S(1)} collective-permute-done((bf16[144,1024]{1,0:T(8,128)(2,1)S(1)}, bf16[144,1024]{1,0:T(8,128)(2,1)S(1)}, u32[]{:S(2)}, u32[]{:S(2)}) %collective-permute-start.10) | collective-permute-done | bytes 294944 | tf_op jit(solution)/shard_map/ppermute | solution.py:747
  65.9 6.8 %collective-permute-start.15 = (bf16[576,256]{1,0:T(8,128)(2,1)}, bf16[576,256]{1,0:T(8,128)(2,1)S(1)}, u32[]{:S(2)}, u32[]{:S(2)}) collective-permute-start(bf16[576,256]{1,0:T(8,128)(2,1)} %maximum_select_fusion.11), channel_id=1, source_target_pairs={{0,1},{1,2},{2,3},{3,0},{4,5},{5,6},{6,7},{7,4},{8,9},{9,10},{10,1... | collective-permute-start | bytes 884744 | tf_op jit(solution)/shard_map/ppermute | solution.py:747
  87.3 8.2 %shard_map.205 = (bf16[1152,1024]{1,0:T(8,128)(2,1)S(1)}, bf16[1152,1024]{1,0:T(8,128)(2,1)}, f32[1152,128]{1,0:T(8,128)S(1)}, f32[8,1024]{1,0:T(8,128)S(1)}, bf...) custom-call(s32[1]{0:T(128)} %bitcast.me_ref, ...), custom_call_target="tpu_custom_call" | custom-call | flops 3623878656 | bytes 12582912 | tf_op jit(solution)/shard_map/pallas_call | solution.py:206
  96.3 3.3 collective-permute-done.16
  108.0 24.9 %shard_map.206 = (bf16[1152,512]{1,0:T(8,128)(2,1)S(1)}, bf16[4,3,1152,768]{3,2,1,0:T(8,128)(2,1)}) custom-call(s32[1]{0:T(128)} %dynamic_slice.85.flag_ref, bf16[1152,512]{1,0:T(8,128)(2,1)S(1)} %get-tuple-element.240.q_ref, bf16[1152,512]{1,0:T(8,128)(2,1)S(1)} %get-tuple-element.241.k_ref, bf16[1152,512]{1,0:T(8,128)(2,1)S(1)} %get-tuple-element.242.v_ref), custom_call_target="tpu_custom_call" | custom-call | flops 10871635968 | bytes 29360128 | tf_op jit(solution)/shard_map/pallas_call | solution.py:277
  139.5 3.0 collective-permute-start.26
  144.9 3.6 collective-permute-done.25
  152.1 4.2 %collective-permute-done.28.other_ref = bf16[4,144,1024]{2,1,0:T(8,128)(2,1)S(1)} collective-permute-done((bf16[4,144,1024]{2,1,0:T(8,128)(2,1)S(1)}, bf16[4,144,1024]{2,1,0:T(8,128)(2,1)S(1)}, u32[]{:S(2)}, u32[]{:S(2)}) %collective-permute-start.28) | collective-permute-done | bytes 1179680 | tf_op jit(solution)/shard_map/ppermute | solution.py:741
  166.9 23.3 %shard_map.209 = (bf16[1152,1024]{1,0:T(8,128)(2,1)}, bf16[1152,1024]{1,0:T(8,128)(2,1)}, bf16[2,2,576,256]{3,2,1,0:T(8,128)(2,1)S(1)}, bf16[2,2,576,256]{3,2,1,...) custom-call(s32[1]{0:T(128)} %bitcast.me_ref, s32[1]{0:T(128)} %bitcast.1.core_ref, ...), custom_call_target="tpu_custom_call" | custom-call | flops 16307453952 | bytes 20971520 | tf_op jit(solution)/shard_map/pallas_call | solution.py:427
  192.3 10.6 %collective-permute-done.32.refs_3_ = bf16[2,480,256]{2,1,0:T(8,128)(2,1)S(1)} collective-permute-done((bf16[2,480,256]{2,1,0:T(8,128)(2,1)S(1)}, bf16[2,480,256]{2,1,0:T(8,128)(2,1)S(1)}, u32[]{:S(2)}, u32[]{:S(2)}) %collective-permute-start.32) | collective-permute-done | bytes 491552 | tf_op jit(solution)/shard_map/ppermute | solution.py:744
  205.4 25.2 %shard_map.210 = (bf16[1152,1024]{1,0:T(8,128)(2,1)}, bf16[1152,1024]{1,0:T(8,128)(2,1)}, bf16[2,2,480,256]{3,2,1,0:T(8,128)(2,1)S(1)}, bf16[2,2,480,256]{3,2,1,...) custom-call(s32[1]{0:T(128)} %bitcast.me_ref, ...), custom_call_target="tpu_custom_call" | custom-call | flops 13589544960 | bytes 20971520 | tf_op jit(solution)/shard_map/pallas_call | solution.py:427
  234.0 3.1 collective-permute-done.37.other_ref
  237.1 7.6 %shard_map.211 = (f32[4,144,1024]{2,1,0:T(8,128)S(1)}, bf16[1152,1024]{1,0:T(8,128)(2,1)S(1)}, bf16[1152,512]{1,0:T(8,128)(2,1)S(1)}, f32[1,1024]{1,0:T(1,128)S(1)}, bf16[4,144,1024]{2,1,0:T(8,128)(2,1)S(1)}) custom-call(s32[1]{0:T(128)} %bitcast.me_ref, s32[1]{0:T(128)} %bitcast.1.core_ref, f32[1152,1024]{1,0:T(8,128)} %copy-done.2, ...), custom_call_target="tpu_custom_call" | custom-call | flops 1207959552 | bytes 23068672 | tf_op jit(solution)/shard_map/pallas_call | solution.py:508
  250.9 3.8 collective-permute-start.43
  256.0 16.4 %shard_map.212 = (bf16[1152,256]{1,0:T(8,128)(2,1)S(1)}, bf16[1152,256]{1,0:T(8,128)(2,1)S(1)}, bf16[1152,256]{1,0:T(8,128)(2,1)S(1)}) custom-call(s32[1]{0:T(128)} %dynamic_slice.85.flag_ref, bf16[1152,512]{1,0:T(8,128)(2,1)S(1)} %copy-done.34, bf16[1152,512]{1,0:T(8,128)(2,1)S(1)} %copy-done.36, bf16[1152,512]{1,0:T(8,128)(2,1)S(1)} %copy-done.38, ...), custom_call_target="tpu_custom_call" | custom-call | flops 10871635968 | bytes 16777216 | tf_op jit(solution)/shard_map/pallas_call | solution.py:591
  278.1 16.0 %shard_map.213 = (bf16[1152,256]{1,0:T(8,128)(2,1)S(1)}, bf16[1152,256]{1,0:T(8,128)(2,1)S(1)}, bf16[1152,256]{1,0:T(8,128)(2,1)S(1)}) custom-call(s32[1]{0:T(128)} %dynamic_slice.85.flag_ref, bf16[1152,512]{1,0:T(8,128)(2,1)S(1)} %copy-done.34, bf16[1152,512]{1,0:T(8,128)(2,1)S(1)} %copy-done.36, bf16[1152,512]{1,0:T(8,128)(2,1)S(1)} %copy-done.38, ...), custom_call_target="tpu_custom_call" | custom-call | flops 10871635968 | bytes 16777216 | tf_op jit(solution)/shard_map/pallas_call | solution.py:591
  298.8 17.9 %shard_map.214 = (bf16[1152,1024]{1,0:T(8,128)(2,1)}, bf16[4,144,1024]{2,1,0:T(8,128)(2,1)}, bf16[2,2,528,256]{3,2,1,0:T(8,128)(2,1)}, bf16[2,2,528,256]{3,2,1,0...) custom-call(s32[1]{0:T(128)} %bitcast.me_ref, s32[1]{0:T(128)} %bitcast.1.core_ref, ...), custom_call_target="tpu_custom_call" | custom-call | flops 8455716864 | bytes 25165824 | tf_op jit(solution)/shard_map/pallas_call | solution.py:670
  332.6 8.5 %collective-permute-done.57 = bf16[480,256]{1,0:T(8,128)(2,1)S(1)} collective-permute-done((bf16[480,256]{1,0:T(8,128)(2,1)}, bf16[480,256]{1,0:T(8,128)(2,1)S(1)}, u32[]{:S(2)}, u32[]{:S(2)}) %collective-permute-start.57) | collective-permute-done | bytes 245792 | tf_op jit(solution)/shard_map/ppermute | solution.py:747
  341.1 5.5 %collective-permute-done.52 = bf16[2,2,528,256]{3,2,1,0:T(8,128)(2,1)S(1)} collective-permute-done((bf16[2,2,528,256]{3,2,1,0:T(8,128)(2,1)}, bf16[2,2,528,256]{3,2,1,0:T(8,128)(2,1)S(1)}, u32[]{:S(2)}, u32[]{:S(2)}) %collective-permute-start.52) | collective-permute-done | bytes 1081376 | tf_op jit(solution)/shard_map/ppermute | solution.py:744
  354.1 11.5 %collective-permute-done.60 = bf16[144,1024]{1,0:T(8,128)(2,1)S(1)} collective-permute-done((bf16[144,1024]{1,0:T(8,128)(2,1)S(1)}, bf16[144,1024]{1,0:T(8,128)(2,1)S(1)}, u32[]{:S(2)}, u32[]{:S(2)}) %collective-permute-start.60) | collective-permute-done | bytes 294944 | tf_op jit(solution)/shard_map/ppermute | solution.py:747
  376.7 14.2 %collective-permute-done.62 = bf16[528,256]{1,0:T(8,128)(2,1)S(1)} collective-permute-done((bf16[528,256]{1,0:T(8,128)(2,1)S(1)}, bf16[528,256]{1,0:T(8,128)(2,1)S(1)}, u32[]{:S(2)}, u32[]{:S(2)}) %collective-permute-start.62) | collective-permute-done | bytes 270368 | tf_op jit(solution)/shard_map/ppermute | solution.py:747
  (370 shorter events, 151.5 us)
Async XLA Ops:
  35.1 27.1 %collective-permute-start.7 = (bf16[4,528,256]{2,1,0:T(8,128)(2,1)S(1)}, bf16[4,528,256]{2,1,0:T(8,128)(2,1)S(1)}, u32[]{:S(2)}, u32[]{:S(2)}) collective-permute-start(bf16[4,528,256]{2,1,0:T(8,128)(2,1)S(1)} %pad_maximum_fusion.6.w0), channel_id=1, source_target_pairs={{0,8},{4,12},{8,0},{12,4},{16,24},{20,28},{24,16},{28,20},{1,9},{5... | collective-permute-start | bytes 3244040 | tf_op jit(solution)/shard_map/ppermute | solution.py:744
  36.7 25.5 %collective-permute-start.8 = (bf16[4,528,256]{2,1,0:T(8,128)(2,1)S(1)}, bf16[4,528,256]{2,1,0:T(8,128)(2,1)S(1)}, u32[]{:S(2)}, u32[]{:S(2)}) collective-permute-start(bf16[4,528,256]{2,1,0:T(8,128)(2,1)S(1)} %pad_maximum_fusion.6.w0), channel_id=1, source_target_pairs={{0,16},{4,20},{8,24},{12,28},{16,0},{20,4},{24,8},{28,12},{1,17},{... | collective-permute-start | bytes 3244040 | tf_op jit(solution)/shard_map/ppermute | solution.py:744
  65.9 30.4 %collective-permute-start.15 = (bf16[576,256]{1,0:T(8,128)(2,1)}, bf16[576,256]{1,0:T(8,128)(2,1)S(1)}, u32[]{:S(2)}, u32[]{:S(2)}) collective-permute-start(bf16[576,256]{1,0:T(8,128)(2,1)} %maximum_select_fusion.11), channel_id=1, source_target_pairs={{0,1},{1,2},{2,3},{3,0},{4,5},{5,6},{6,7},{7,4},{8,9},{9,10},{10,1... | collective-permute-start | bytes 884744 | tf_op jit(solution)/shard_map/ppermute | solution.py:747
  72.7 23.6 %collective-permute-start.17 = (bf16[576,256]{1,0:T(8,128)(2,1)}, bf16[576,256]{1,0:T(8,128)(2,1)S(1)}, u32[]{:S(2)}, u32[]{:S(2)}) collective-permute-start(bf16[576,256]{1,0:T(8,128)(2,1)} %maximum_select_fusion.11), channel_id=1, source_target_pairs={{0,3},{1,0},{2,1},{3,2},{4,7},{5,4},{6,5},{7,6},{8,11},{9,8},{10,9... | collective-permute-start | bytes 884744 | tf_op jit(solution)/shard_map/ppermute | solution.py:747
  75.0 24.5 %collective-permute-start.16 = (bf16[576,256]{1,0:T(8,128)(2,1)}, bf16[576,256]{1,0:T(8,128)(2,1)S(1)}, u32[]{:S(2)}, u32[]{:S(2)}) collective-permute-start(bf16[576,256]{1,0:T(8,128)(2,1)} %maximum_select_fusion.11), channel_id=1, source_target_pairs={{0,2},{1,3},{2,0},{3,1},{4,6},{5,7},{6,4},{7,5},{8,10},{9,11},{10,... | collective-permute-start | bytes 884744 | tf_op jit(solution)/shard_map/ppermute | solution.py:747
  99.8 36.2 %collective-permute-start.18 = (bf16[4,576,256]{2,1,0:T(8,128)(2,1)S(1)}, bf16[4,576,256]{2,1,0:T(8,128)(2,1)S(1)}, u32[]{:S(2)}, u32[]{:S(2)}) collective-permute-start(bf16[4,576,256]{2,1,0:T(8,128)(2,1)S(1)} %pad_maximum_fusion.1.refs_0_), channel_id=1, source_target_pairs={{0,8},{4,12},{8,0},{12,4},{16,24},{20,28},{24,16},{28,20},{1,9},{5... | collective-permute-start | bytes 3538952 | tf_op jit(solution)/shard_map/ppermute | solution.py:744
  101.3 34.7 %collective-permute-start.19 = (bf16[4,576,256]{2,1,0:T(8,128)(2,1)S(1)}, bf16[4,576,256]{2,1,0:T(8,128)(2,1)S(1)}, u32[]{:S(2)}, u32[]{:S(2)}) collective-permute-start(bf16[4,576,256]{2,1,0:T(8,128)(2,1)S(1)} %pad_maximum_fusion.1.refs_0_), channel_id=1, source_target_pairs={{0,16},{4,20},{8,24},{12,28},{16,0},{20,4},{24,8},{28,12},{1,17},{... | collective-permute-start | bytes 3538952 | tf_op jit(solution)/shard_map/ppermute | solution.py:744
  102.8 33.2 %collective-permute-start.20 = (bf16[144,1024]{1,0:T(8,128)(2,1)S(1)}, bf16[144,1024]{1,0:T(8,128)(2,1)S(1)}, u32[]{:S(2)}, u32[]{:S(2)}) collective-permute-start(bf16[144,1024]{1,0:T(8,128)(2,1)S(1)} %copy-done.67), channel_id=1, source_target_pairs={{0,1},{1,2},{2,3},{3,0},{4,5},{5,6},{6,7},{7,4},{8,9},{9,10},{10,1... | collective-permute-start | bytes 884744 | tf_op jit(solution)/shard_map/ppermute | solution.py:747
  105.5 30.5 %collective-permute-start.21 = (bf16[144,1024]{1,0:T(8,128)(2,1)S(1)}, bf16[144,1024]{1,0:T(8,128)(2,1)S(1)}, u32[]{:S(2)}, u32[]{:S(2)}) collective-permute-start(bf16[144,1024]{1,0:T(8,128)(2,1)S(1)} %copy-done.66), channel_id=1, source_target_pairs={{0,2},{1,3},{2,0},{3,1},{4,6},{5,7},{6,4},{7,5},{8,10},{9,11},{10,... | collective-permute-start | bytes 884744 | tf_op jit(solution)/shard_map/ppermute | solution.py:747
  107.2 28.8 %collective-permute-start.22 = (bf16[144,1024]{1,0:T(8,128)(2,1)S(1)}, bf16[144,1024]{1,0:T(8,128)(2,1)S(1)}, u32[]{:S(2)}, u32[]{:S(2)}) collective-permute-start(bf16[144,1024]{1,0:T(8,128)(2,1)S(1)} %copy-done.65), channel_id=1, source_target_pairs={{0,3},{1,0},{2,1},{3,2},{4,7},{5,4},{6,5},{7,6},{8,11},{9,8},{10,9... | collective-permute-start | bytes 884744 | tf_op jit(solution)/shard_map/ppermute | solution.py:747
  164.7 25.5 %collective-permute-start.30 = (bf16[4,480,256]{2,1,0:T(8,128)(2,1)S(1)}, bf16[4,480,256]{2,1,0:T(8,128)(2,1)S(1)}, u32[]{:S(2)}, u32[]{:S(2)}) collective-permute-start(bf16[4,480,256]{2,1,0:T(8,128)(2,1)S(1)} %pad_maximum_fusion.7.refs_0_), channel_id=1, source_target_pairs={{0,8},{4,12},{8,0},{12,4},{16,24},{20,28},{24,16},{28,20},{1,9},{5... | collective-permute-start | bytes 2949128 | tf_op jit(solution)/shard_map/ppermute | solution.py:744
  165.9 24.3 %collective-permute-start.31 = (bf16[4,480,256]{2,1,0:T(8,128)(2,1)S(1)}, bf16[4,480,256]{2,1,0:T(8,128)(2,1)S(1)}, u32[]{:S(2)}, u32[]{:S(2)}) collective-permute-start(bf16[4,480,256]{2,1,0:T(8,128)(2,1)S(1)} %pad_maximum_fusion.7.refs_0_), channel_id=1, source_target_pairs={{0,16},{4,20},{8,24},{12,28},{16,0},{20,4},{24,8},{28,12},{1,17},{... | collective-permute-start | bytes 2949128 | tf_op jit(solution)/shard_map/ppermute | solution.py:744
  203.7 26.9 %collective-permute-start.34 = (bf16[2,2,576,256]{3,2,1,0:T(8,128)(2,1)S(1)}, bf16[2,2,576,256]{3,2,1,0:T(8,128)(2,1)S(1)}, u32[]{:S(2)}, u32[]{:S(2)}) collective-permute-start(bf16[2,2,576,256]{3,2,1,0:T(8,128)(2,1)S(1)} %get-tuple-element.300), channel_id=1, source_target_pairs={{0,8},{4,12},{8,0},{12,4},{16,24},{20,28},{24,16},{28,20},{1,9},{5... | collective-permute-start | bytes 3538952 | tf_op jit(solution)/shard_map/ppermute | solution.py:744
  204.4 26.2 %collective-permute-start.35 = (bf16[2,2,576,256]{3,2,1,0:T(8,128)(2,1)S(1)}, bf16[2,2,576,256]{3,2,1,0:T(8,128)(2,1)S(1)}, u32[]{:S(2)}, u32[]{:S(2)}) collective-permute-start(bf16[2,2,576,256]{3,2,1,0:T(8,128)(2,1)S(1)} %get-tuple-element.301), channel_id=1, source_target_pairs={{0,16},{4,20},{8,24},{12,28},{16,0},{20,4},{24,8},{28,12},{1,17},{... | collective-permute-start | bytes 3538952 | tf_op jit(solution)/shard_map/ppermute | solution.py:744
  247.7 25.5 %collective-permute-start.40 = (bf16[2,2,480,256]{3,2,1,0:T(8,128)(2,1)S(1)}, bf16[2,2,480,256]{3,2,1,0:T(8,128)(2,1)S(1)}, u32[]{:S(2)}, u32[]{:S(2)}) collective-permute-start(bf16[2,2,480,256]{3,2,1,0:T(8,128)(2,1)S(1)} %get-tuple-element.326), channel_id=1, source_target_pairs={{0,8},{4,12},{8,0},{12,4},{16,24},{20,28},{24,16},{28,20},{1,9},{5... | collective-permute-start | bytes 2949128 | tf_op jit(solution)/shard_map/ppermute | solution.py:744
  249.0 24.3 %collective-permute-start.41 = (bf16[2,2,480,256]{3,2,1,0:T(8,128)(2,1)S(1)}, bf16[2,2,480,256]{3,2,1,0:T(8,128)(2,1)S(1)}, u32[]{:S(2)}, u32[]{:S(2)}) collective-permute-start(bf16[2,2,480,256]{3,2,1,0:T(8,128)(2,1)S(1)} %get-tuple-element.328), channel_id=1, source_target_pairs={{0,16},{4,20},{8,24},{12,28},{16,0},{20,4},{24,8},{28,12},{1,17},{... | collective-permute-start | bytes 2949128 | tf_op jit(solution)/shard_map/ppermute | solution.py:744
  250.9 22.3 %collective-permute-start.42 = (bf16[144,1024]{1,0:T(8,128)(2,1)S(1)}, bf16[144,1024]{1,0:T(8,128)(2,1)S(1)}, u32[]{:S(2)}, u32[]{:S(2)}) collective-permute-start(bf16[144,1024]{1,0:T(8,128)(2,1)S(1)} %get-tuple-element.418), channel_id=1, source_target_pairs={{0,1},{1,2},{2,3},{3,0},{4,5},{5,6},{6,7},{7,4},{8,9},{9,10},{10,1... | collective-permute-start | bytes 884744 | tf_op jit(solution)/shard_map/ppermute | solution.py:747
  250.9 22.3 %collective-permute-start.43 = (bf16[144,1024]{1,0:T(8,128)(2,1)S(1)}, bf16[144,1024]{1,0:T(8,128)(2,1)S(1)}, u32[]{:S(2)}, u32[]{:S(2)}) collective-permute-start(bf16[144,1024]{1,0:T(8,128)(2,1)S(1)} %get-tuple-element.417), channel_id=1, source_target_pairs={{0,3},{1,0},{2,1},{3,2},{4,7},{5,4},{6,5},{7,6},{8,11},{9,8},{10,9... | collective-permute-start | bytes 884744 | tf_op jit(solution)/shard_map/ppermute | solution.py:747
  254.7 39.5 %collective-permute-start.46 = (bf16[144,1024]{1,0:T(8,128)(2,1)S(1)}, bf16[144,1024]{1,0:T(8,128)(2,1)S(1)}, u32[]{:S(2)}, u32[]{:S(2)}) collective-permute-start(bf16[144,1024]{1,0:T(8,128)(2,1)S(1)} %get-tuple-element.415), channel_id=1, source_target_pairs={{0,2},{1,3},{2,0},{3,1},{4,6},{5,7},{6,4},{7,5},{8,10},{9,11},{10,... | collective-permute-start | bytes 884744 | tf_op jit(solution)/shard_map/ppermute | solution.py:747
  320.4 26.2 %collective-permute-start.52 = (bf16[2,2,528,256]{3,2,1,0:T(8,128)(2,1)}, bf16[2,2,528,256]{3,2,1,0:T(8,128)(2,1)S(1)}, u32[]{:S(2)}, u32[]{:S(2)}) collective-permute-start(bf16[2,2,528,256]{3,2,1,0:T(8,128)(2,1)} %get-tuple-element.367), channel_id=1, source_target_pairs={{0,8},{4,12},{8,0},{12,4},{16,24},{20,28},{24,16},{28,20},{1,9},{5... | collective-permute-start | bytes 3244040 | tf_op jit(solution)/shard_map/ppermute | solution.py:744
  321.6 25.9 %collective-permute-start.53 = (bf16[2,2,528,256]{3,2,1,0:T(8,128)(2,1)}, bf16[2,2,528,256]{3,2,1,0:T(8,128)(2,1)S(1)}, u32[]{:S(2)}, u32[]{:S(2)}) collective-permute-start(bf16[2,2,528,256]{3,2,1,0:T(8,128)(2,1)} %get-tuple-element.368), channel_id=1, source_target_pairs={{0,16},{4,20},{8,24},{12,28},{16,0},{20,4},{24,8},{28,12},{1,17},{... | collective-permute-start | bytes 3244040 | tf_op jit(solution)/shard_map/ppermute | solution.py:744
  341.1 28.9 %collective-permute-start.64 = (bf16[2,144,1024]{2,1,0:T(8,128)(2,1)S(1)}, bf16[2,144,1024]{2,1,0:T(8,128)(2,1)S(1)}, u32[]{:S(2)}, u32[]{:S(2)}) collective-permute-start(bf16[2,144,1024]{2,1,0:T(8,128)(2,1)S(1)} %maximum_select_fusion.5), channel_id=1, source_target_pairs={{0,4},{4,0},{8,12},{12,8},{16,20},{20,16},{24,28},{28,24},{1,5},{5... | collective-permute-start | bytes 1769480 | tf_op jit(solution)/shard_map/ppermute | solution.py:741
  368.7 22.1 %collective-permute-start.62 = (bf16[528,256]{1,0:T(8,128)(2,1)S(1)}, bf16[528,256]{1,0:T(8,128)(2,1)S(1)}, u32[]{:S(2)}, u32[]{:S(2)}) collective-permute-start(bf16[528,256]{1,0:T(8,128)(2,1)S(1)} %get-tuple-element.441), channel_id=1, source_target_pairs={{0,2},{1,3},{2,0},{3,1},{4,6},{5,7},{6,4},{7,5},{8,10},{9,11},{10,... | collective-permute-start | bytes 811016 | tf_op jit(solution)/shard_map/ppermute | solution.py:747
  368.8 22.1 %collective-permute-start.63 = (bf16[528,256]{1,0:T(8,128)(2,1)S(1)}, bf16[528,256]{1,0:T(8,128)(2,1)S(1)}, u32[]{:S(2)}, u32[]{:S(2)}) collective-permute-start(bf16[528,256]{1,0:T(8,128)(2,1)S(1)} %get-tuple-element.440), channel_id=1, source_target_pairs={{0,1},{1,2},{2,3},{3,0},{4,5},{5,6},{6,7},{7,4},{8,9},{9,10},{10,1... | collective-permute-start | bytes 811016 | tf_op jit(solution)/shard_map/ppermute | solution.py:747
  (123 other events, 1306.5 us)
